TPU v7x, 256 devices: a whole 4x4x8 slice. The times are simulated.
256 devices in a mesh: context: 16 (over x, y), tensor: 16 (over z, core).
Axes of the slice: x: 4, y: 4, z: 8, core: 2. Of those that a mesh axis runs over, the one named last changes fastest.
Arguments:
- query_rows: bfloat16 [2048, 8192], P('context', 'tensor'), may hold values from -6 to 6
- key_rows: bfloat16 [2048, 8192], P('context', 'tensor'), may hold values from -6 to 6
- value_rows: bfloat16 [2048, 8192], P('context', 'tensor'), may hold values from -6 to 6
- residue: float32 [16, 8192], P(None, 'tensor'), may hold values from -3 to 3
- decay_rate: float32 [16, 8192], P(None, 'tensor'), may hold values from 9.765625e-05 to 0.04
- out_weight: bfloat16 [8192, 8192], P('tensor'), may hold values from -0.09375 to 0.09375
- cotangent: bfloat16 [2048, 8192], P('context', 'tensor'), may hold values from -6 to 6
Outputs:
- mixed_out: bfloat16 [2048, 8192], P('context', 'tensor')
- query_grad: bfloat16 [2048, 8192], P('context', 'tensor')
- key_grad: bfloat16 [2048, 8192], P('context', 'tensor')
- value_grad: bfloat16 [2048, 8192], P('context', 'tensor')
- weight_grad: bfloat16 [8192, 8192], P('tensor', 'context')
All inputs are finite; a program needn't handle non-finite values.
Results may differ from a plain program's by a relative error of at most 0.027.
Values may be sent and summed in bfloat16 or wider, within the bound.
A program may use at most 128 MiB of HBM per device.

v0:
```python
import functools
import math

import jax
import jax.numpy as jnp
from jax import lax
from jax.experimental import pallas as pl
from jax.experimental.pallas import tpu as pltpu
from jax.sharding import PartitionSpec as P

MESH = pl.DeviceIdType.MESH
F32 = jnp.float32
BF16 = jnp.bfloat16
LANES = 128


def body(
    X, Y, Z,
    q_ref, k_ref, v_ref, res_ref, dec_ref, w_ref, cot_ref,
    mixed_ref, qg_ref, kg_ref, vg_ref, wg_ref,
    wv, cot_all, cot_t, gat, part, sib, rs_out, rs_in, st_f, st_g,
    src, cgr, conv, back, mix, kpad, krev, wacc, rates, weights, steps, starts,
    w_sem, ag_ss, ag_rs, cs_ss, cs_rs, aa_ss, aa_rs, fw_ss, fw_rs, st_ss, st_rs,
    g1_ss, g1_rs, g2_ss, g2_rs, sb_ss, sb_rs, rr_ss, rr_rs,
):
    N = X * Y
    R, C = q_ref.shape
    M = dec_ref.shape[0]
    T = R // 8
    G = C // LANES
    H = Z // 2
    c = lax.axis_index("context")
    j = lax.axis_index("tensor")
    z, r = j // 2, j % 2
    cx, cy = c // Y, c % Y
    other = z * 2 + 1 - r
    mine = (c, j)
    sibling = (c, other)
    zdev = [(c, ((z + 1) % Z) * 2 + r), (c, ((z + Z - 1) % Z) * 2 + r)]
    xdev = [(((cx + 1) % X) * Y + cy, j), (((cx + X - 1) % X) * Y + cy, j)]
    ydev = [(cx * Y + (cy + 1) % Y, j), (cx * Y + (cy + Y - 1) % Y, j)]

    def copy(source, target, send_sem, recv_sem, device):
        return pltpu.make_async_remote_copy(
            src_ref=source, dst_ref=target, send_sem=send_sem, recv_sem=recv_sem,
            device_id=device, device_id_type=MESH,
        )

    def lanes_of(g):
        return pl.ds(pl.multiple_of(g * LANES, LANES), LANES)

    def w_copy(n):
        return pltpu.make_async_copy(
            w_ref.at[:, pl.ds(pl.multiple_of(n * C, LANES), C)], wv.at[n], w_sem.at[n]
        )

    @pl.loop(0, 2 * Z)
    def _(n):
        w_copy(n).start()

    barrier = pltpu.get_barrier_semaphore()
    for device in zdev + [sibling]:
        pl.semaphore_signal(barrier, inc=1, device_id=device, device_id_type=MESH)

    @pl.loop(0, N)
    def _(p):
        @pl.when(p != c)
        def _():
            pl.semaphore_signal(barrier, inc=1, device_id=(p, j), device_id_type=MESH)

    rows8 = lax.broadcasted_iota(jnp.int32, (8, LANES), 0).astype(F32)

    def spread_modes():
        weight = res_ref[...] * jnp.sqrt(dec_ref[...])
        for m in range(M):
            rate = jnp.broadcast_to(dec_ref[pl.ds(m, 1), :], (8, C))
            rates[m] = rate
            steps[m] = jnp.exp(-8.0 * rate)
            weights[m] = jnp.broadcast_to(weight[m : m + 1], (8, C))

    def local_states(values, forward, out, place):
        @pl.loop(0, G)
        def _(g):
            lanes = lanes_of(g)
            tiles = [values[pl.ds(8 * a, 8), lanes] for a in range(T)]
            if not forward:
                tiles = tiles[::-1]

            @pl.loop(0, M // 8)
            def _(eight):
                sums = []
                for inner in range(8):
                    m = eight * 8 + inner
                    step = steps[m, :, lanes]
                    total = tiles[0]
                    for tile in tiles[1:]:
                        total = total * step + tile
                    reach = 7.0 - rows8 if forward else rows8
                    total = total * jnp.exp(-rates[m, :, lanes] * reach)
                    sums.append(jnp.sum(total, axis=0, keepdims=True))
                modes = pl.ds(pl.multiple_of(eight * 8, 8), 8)
                out[place, modes, lanes] = jnp.concatenate(sums, axis=0)

    def filter_tables():
        kpad[pl.ds(0, 8), :] = jnp.zeros((8, C), F32)
        krev[pl.ds(R, 8), :] = jnp.zeros((8, C), F32)

        @pl.loop(0, G)
        def _(g):
            lanes = lanes_of(g)

            def add_mode(m, tiles):
                rate, weight, step = rates[m, :, lanes], weights[m, :, lanes], steps[m, :, lanes]
                ahead = weight * jnp.exp(-rate * rows8)
                behind = weight * jnp.exp(-rate * (7.0 - rows8))
                new = []
                for a in range(T):
                    new.append((tiles[a][0] + ahead, tiles[a][1] + behind))
                    ahead = ahead * step
                    behind = behind * step
                return tuple(new)

            zero = jnp.zeros((8, LANES), F32)
            tiles = lax.fori_loop(0, M, add_mode, tuple((zero, zero) for _ in range(T)))
            for a in range(T):
                kpad[pl.ds(8 + 8 * a, 8), lanes] = tiles[a][0]
                krev[pl.ds(8 * (T - 1 - a), 8), lanes] = tiles[a][1]

    def toeplitz(values, forward, out):
        @pl.loop(0, G)
        def _(g):
            lanes = lanes_of(g)
            total = [jnp.zeros((8, LANES), F32) for _ in range(T)]
            for b in range(8):
                if forward:
                    taps = [kpad[pl.ds(8 + 8 * n - b, 8), lanes] for n in range(T)]
                else:
                    taps = [krev[pl.ds(R - 1 - 8 * n - b, 8), lanes] for n in range(T)]
                for u in range(T):
                    row = jnp.broadcast_to(values[pl.ds(8 * u + b, 1), lanes], (8, LANES))
                    for a in range(u, T) if forward else range(u + 1):
                        total[a] = total[a] + taps[abs(a - u)] * row
            for a in range(T):
                out[pl.ds(8 * a, 8), lanes] = total[a]

    def carry_in(states, forward):
        decay = jnp.exp(-float(R) * dec_ref[...])

        def step(n, total):
            p = n if forward else N - 1 - n
            return total * decay + states[p]

        count = c if forward else N - 1 - c
        total = lax.fori_loop(0, count, step, jnp.zeros((M, C), F32))
        for m in range(M):
            starts[m] = weights[m] * total[m : m + 1]

    def add_carry(forward, out):
        @pl.loop(0, G)
        def _(g):
            lanes = lanes_of(g)

            def add_mode(m, tiles):
                rate, step = rates[m, :, lanes], steps[m, :, lanes]
                term = starts[m, :, lanes] * jnp.exp(-rate * ((rows8 + 1.0) if forward else (8.0 - rows8)))
                new = []
                for a in range(T):
                    new.append(tiles[a] + term)
                    term = term * step
                return tuple(new)

            order = list(range(T)) if forward else list(range(T))[::-1]
            tiles = lax.fori_loop(
                0, M, add_mode, tuple(out[pl.ds(8 * a, 8), lanes] for a in order)
            )
            for n, a in enumerate(order):
                out[pl.ds(8 * a, 8), lanes] = tiles[n]

    def state_copy(states, way, p, owner):
        return copy(
            states.at[owner], states.at[owner], st_ss.at[way, p], st_rs.at[way, owner], (p, j)
        )

    def send_states(states, way):
        lo, hi = (c + 1, N) if way == 0 else (0, c)

        @pl.loop(lo, hi)
        def _(p):
            state_copy(states, way, p, c).start()

    def wait_states(states, way):
        lo, hi = (0, c) if way == 0 else (c + 1, N)

        @pl.loop(lo, hi)
        def _(p):
            state_copy(states, way, c, p).wait_recv()

    def drain_states(states, way):
        lo, hi = (c + 1, N) if way == 0 else (0, c)

        @pl.loop(lo, hi)
        def _(p):
            state_copy(states, way, p, c).wait_send()

    def piece(way, hop, last, size):
        if hop < last:
            return pl.ds(0, size)
        return pl.ds(way * (size // 2), size // 2)

    def ag_copy(way, hop, sending):
        away = hop - 1 if sending else hop
        owner = (z - away + Z) % Z if way == 0 else (z + away) % Z
        rows = piece(way, hop, H, R)
        ref = cot_all.at[owner * 2 + r, rows]
        return copy(ref, ref, ag_ss.at[way, hop - 1], ag_rs.at[way, hop - 1], zdev[way])

    def cs_copy(zz, sending):
        ref = cot_all.at[zz * 2 + (r if sending else 1 - r)]
        return copy(ref, ref, cs_ss.at[zz], cs_rs.at[zz], sibling)

    def aa_copy(zz):
        owner = zz * 2 + r
        return copy(
            cot_all.at[owner], cot_t.at[cx, cy], aa_ss.at[zz], aa_rs.at[c], (owner, j)
        )

    def spread(zz):
        cs_copy(zz, True).start()

        @pl.when(zz * 2 + r != c)
        def _():
            aa_copy(zz).start()

    def ag_send(hop):
        for way in range(2):
            ag_copy(way, hop, True).start()

    def ag_arrive(hop):
        for way in range(2):
            ag_copy(way, hop, False).wait_recv()
        if hop < H:
            ag_send(hop + 1)
            spread((z - hop + Z) % Z)
        spread((z + hop) % Z)

    half = R // 2

    def g1_copy(part_at, way, hop, sending):
        size, last, devices, at = (X, X // 2, xdev, cx) if part_at == 0 else (Y, Y // 2, ydev, cy)
        away = hop - 1 if sending else hop
        owner = (at - away + size) % size if way == 0 else (at + away) % size
        low = part_at * half
        if hop == last:
            rows = pl.ds(low + way * (half // 2), half // 2)
        else:
            rows = pl.ds(low, half)
        ref = gat.at[owner, cy, rows] if part_at == 0 else gat.at[cx, owner, rows]
        return copy(ref, ref, g1_ss.at[part_at, way, hop - 1], g1_rs.at[part_at, way, hop - 1], devices[way])

    def g2_copy(part_at, way, hop, sending):
        size, last, devices, at, many = (
            (Y, Y // 2, ydev, cy, X) if part_at == 0 else (X, X // 2, xdev, cx, Y)
        )
        away = hop - 1 if sending else hop
        owner = (at - away + size) % size if way == 0 else (at + away) % size
        group = piece(way, hop, last, many)
        rows = pl.ds(part_at * half, half)
        ref = gat.at[group, owner, rows] if part_at == 0 else gat.at[owner, group, rows]
        return copy(ref, ref, g2_ss.at[part_at, way, hop - 1], g2_rs.at[part_at, way, hop - 1], devices[way])

    def hops_of(phase, part_at):
        return (X // 2, Y // 2)[part_at if phase == 1 else 1 - part_at]

    def gather_send(phase, hop):
        make = g1_copy if phase == 1 else g2_copy
        for part_at in range(2):
            if hop <= hops_of(phase, part_at):
                for way in range(2):
                    make(part_at, way, hop, True).start()

    def gather_wait(phase, hop):
        make = g1_copy if phase == 1 else g2_copy
        for part_at in range(2):
            if hop <= hops_of(phase, part_at):
                for way in range(2):
                    make(part_at, way, hop, False).wait_recv()

    def sb_copy(zz, sending):
        target = zz * 2 + (1 - r if sending else r)
        return copy(part.at[target], sib.at[zz], sb_ss.at[zz], sb_rs.at[zz], sibling)

    def project(lo, hi):
        @pl.loop(lo, hi)
        def _(o):
            hop = H - (o + 1) // 2
            zz = (z + Z + hop * (2 * (o % 2) - 1)) % Z
            gated = gat[cx, cy]
            for core in range(2):
                target = zz * 2 + ((1 - r) if core == 0 else r)
                part[target] = jnp.dot(
                    gated, wv[target], preferred_element_type=F32
                ).astype(BF16)
                if core == 0:
                    sb_copy(zz, True).start()

    def rr_copy(way, step):
        rows = pl.ds(way * half, half) if step == 0 else pl.ds(0, R)
        return copy(
            rs_out.at[way, step, rows], rs_in.at[way, step, rows],
            rr_ss.at[way, step], rr_rs.at[way, step], zdev[way],
        )

    def pair_sum(zz):
        return part[zz * 2 + r].astype(F32) + sib[zz].astype(F32)

    def reduce_step(step):
        if step == 0:
            zz = (z + H) % Z
            sb_copy(zz, False).wait_recv()
            total = pair_sum(zz).astype(BF16)
            for way in range(2):
                rows = slice(way * half, (way + 1) * half)
                rs_out[way, 0, rows] = total[rows]
                rr_copy(way, 0).start()
            return
        for way in range(2):
            away = H - step
            zz = (z + away) % Z if way == 0 else (z - away + Z) % Z
            sb_copy(zz, False).wait_recv()
            rr_copy(way, step - 1).wait_recv()
            add_arrived(way, step, pair_sum(zz), rs_out.at[way, step])
            rr_copy(way, step).start()

    def add_arrived(way, step, total, out):
        if step == 1:
            for part_at in range(2):
                rows = slice(part_at * half, (part_at + 1) * half)
                value = total[rows]
                if part_at == way:
                    value = value + rs_in[way, 0, rows].astype(F32)
                out[rows] = value.astype(BF16)
        else:
            out[...] = (total + rs_in[way, step - 1].astype(F32)).astype(BF16)

    def reduce_last():
        sb_copy(z, False).wait_recv()
        for way in range(2):
            rr_copy(way, H - 1).wait_recv()
        total = pair_sum(z)
        if H == 1:
            for way in range(2):
                rows = slice(way * half, (way + 1) * half)
                mixed_ref[rows] = (total[rows] + rs_in[way, 0, rows].astype(F32)).astype(BF16)
        else:
            total = total + rs_in[0, H - 1].astype(F32) + rs_in[1, H - 1].astype(F32)
            mixed_ref[...] = total.astype(BF16)

    spread_modes()
    src[...] = k_ref[...].astype(F32) * v_ref[...].astype(F32)
    cot_all[j] = cot_ref[...]
    local_states(src, True, st_f, c)
    pl.semaphore_wait(barrier, N - 1 + 3)
    ag_send(1)
    send_states(st_f, 0)
    spread(z)
    filter_tables()
    toeplitz(src, True, conv)
    if H > 1:
        ag_arrive(1)
    wait_states(st_f, 0)
    carry_in(st_f, True)
    add_carry(True, conv)
    gat[cx, cy] = (q_ref[...].astype(F32) * conv[...]).astype(BF16)
    gather_send(1, 1)
    if H > 2:
        ag_arrive(2)

    @pl.loop(0, 2 * Z)
    def _(n):
        w_copy(n).wait()

    project(0, min(3, Z))
    reduce_step(0)
    gather_wait(1, 1)
    top = max(X // 2, Y // 2)
    for hop in range(2, top + 1):
        gather_send(1, hop)
    if H > 3:
        ag_arrive(3)
    project(min(3, Z), Z)
    for hop in range(2, top + 1):
        gather_wait(1, hop)
    gather_send(2, 1)
    if H > 1:
        reduce_step(1)
    ag_arrive(H)
    @pl.loop(0, Z)
    def _(zz):
        cs_copy(zz, False).wait_recv()

    back[...] = jnp.zeros((R, C), F32)

    @pl.loop(0, 2 * Z)
    def _(n):
        back[...] += lax.dot_general(
            cot_all[n], wv[n], (((1,), (1,)), ((), ())), preferred_element_type=F32
        )

    if H > 2:
        reduce_step(2)
    qg_ref[...] = (back[...] * conv[...]).astype(BF16)
    cgr[...] = back[...] * q_ref[...].astype(F32)
    local_states(cgr, False, st_g, c)
    send_states(st_g, 1)
    gather_wait(2, 1)
    for hop in range(2, top + 1):
        gather_send(2, hop)
    toeplitz(cgr, False, mix)
    if H > 3:
        reduce_step(3)
    for step in range(4, H):
        reduce_step(step)
    active = c % 2 == r

    def fw_copy(p):
        ref = cot_t.at[p // Y, p % Y]
        return copy(ref, ref, fw_ss.at[p], fw_rs.at[p], sibling)

    def each_other(act):
        @pl.loop(0, N)
        def _(p):
            @pl.when(p != c)
            def _():
                act(p)

    def forward_one(p):
        copy(
            cot_all.at[p], cot_t.at[p // Y, p % Y], aa_ss.at[0], aa_rs.at[p], mine
        ).wait_recv()
        fw_copy(p).start()

    @pl.when(active)
    def _():
        each_other(forward_one)

    wait_states(st_g, 1)
    carry_in(st_g, False)
    add_carry(False, mix)
    kg_ref[...] = (mix[...] * v_ref[...].astype(F32)).astype(BF16)
    vg_ref[...] = (mix[...] * k_ref[...].astype(F32)).astype(BF16)
    reduce_last()

    @pl.when(jnp.logical_not(active))
    def _():
        each_other(lambda p: fw_copy(p).wait_recv())

    cot_t[cx, cy] = cot_all[c]
    for hop in range(2, top + 1):
        gather_wait(2, hop)
    wacc[...] = jnp.zeros((C, C), F32)

    @pl.loop(0, X)
    def _(n):
        wacc[...] += lax.dot_general(
            gat[n].reshape(Y * R, C), cot_t[n].reshape(Y * R, C),
            (((0,), (0,)), ((), ())), preferred_element_type=F32,
        )

    wg_ref[...] = wacc[...].astype(BF16)

    drain_states(st_f, 0)
    drain_states(st_g, 1)
    for way in range(2):
        for hop in range(1, H + 1):
            ag_copy(way, hop, True).wait_send()
            rr_copy(way, hop - 1).wait_send()
        for phase, make in ((1, g1_copy), (2, g2_copy)):
            for part_at in range(2):
                for hop in range(1, hops_of(phase, part_at) + 1):
                    make(part_at, way, hop, True).wait_send()

    @pl.loop(0, Z)
    def _(zz):
        cs_copy(zz, True).wait_send()
        sb_copy(zz, True).wait_send()

        @pl.when(zz * 2 + r != c)
        def _():
            aa_copy(zz).wait_send()

    @pl.when(active)
    def _():
        each_other(lambda p: fw_copy(p).wait_send())


def solution(mesh):
    N = mesh.shape["context"]
    X = math.isqrt(N)
    Y = N // X
    Z = mesh.shape["tensor"] // 2
    H = Z // 2

    def shards(query_rows, key_rows, value_rows, residue, decay_rate, out_weight, cotangent):
        R, C = query_rows.shape
        M = residue.shape[0]
        small = jax.ShapeDtypeStruct((R, C), BF16)
        vmem = pl.BlockSpec(memory_space=pltpu.VMEM)
        dma = pltpu.SemaphoreType.DMA
        top = max(X // 2, Y // 2)
        return pl.pallas_call(
            functools.partial(body, X, Y, Z),
            out_shape=(small, small, small, small, jax.ShapeDtypeStruct((C, C), BF16)),
            in_specs=[vmem] * 5 + [pl.BlockSpec(memory_space=pl.ANY), vmem],
            out_specs=(vmem,) * 5,
            scratch_shapes=[
                pltpu.VMEM((2 * Z, C, C), BF16),
                pltpu.VMEM((2 * Z, R, C), BF16),
                pltpu.VMEM((X, Y, R, C), BF16),
                pltpu.VMEM((X, Y, R, C), BF16),
                pltpu.VMEM((2 * Z, R, C), BF16),
                pltpu.VMEM((Z, R, C), BF16),
                pltpu.VMEM((2, H, R, C), BF16),
                pltpu.VMEM((2, H, R, C), BF16),
                pltpu.VMEM((N, M, C), F32),
                pltpu.VMEM((N, M, C), F32),
                pltpu.VMEM((R, C), F32),
                pltpu.VMEM((R, C), F32),
                pltpu.VMEM((R, C), F32),
                pltpu.VMEM((R, C), F32),
                pltpu.VMEM((R, C), F32),
                pltpu.VMEM((R + 8, C), F32),
                pltpu.VMEM((R + 8, C), F32),
                pltpu.VMEM((C, C), F32),
                pltpu.VMEM((M, 8, C), F32),
                pltpu.VMEM((M, 8, C), F32),
                pltpu.VMEM((M, 8, C), F32),
                pltpu.VMEM((M, 8, C), F32),
                dma((2 * Z,)),
                dma((2, H)),
                dma((2, H)),
                dma((Z,)),
                dma((Z,)),
                dma((Z,)),
                dma((N,)),
                dma((N,)),
                dma((N,)),
                dma((2, N)),
                dma((2, N)),
                dma((2, 2, top)),
                dma((2, 2, top)),
                dma((2, 2, top)),
                dma((2, 2, top)),
                dma((Z,)),
                dma((Z,)),
                dma((2, H)),
                dma((2, H)),
            ],
            compiler_params=pltpu.CompilerParams(
                collective_id=0, has_side_effects=True, vmem_limit_bytes=56 * 1024 * 1024
            ),
            name="hyena_block",
        )(query_rows, key_rows, value_rows, residue, decay_rate, out_weight, cotangent)

    placed = (
        P("context", "tensor"),
        P("context", "tensor"),
        P("context", "tensor"),
        P(None, "tensor"),
        P(None, "tensor"),
        P("tensor", None),
        P("context", "tensor"),
    )
    return jax.shard_map(
        shards,
        mesh=mesh,
        in_specs=placed,
        out_specs=(
            P("context", "tensor"),
            P("context", "tensor"),
            P("context", "tensor"),
            P("context", "tensor"),
            P("tensor", "context"),
        ),
        check_vma=False,
    )
```

profile of v0, /device:TPU:64, one launch (start us, length us, event | category | flops | bytes accessed | tf_op | source)
XLA Modules:
  0.0 77.0 jit_solution(3477959754206562540)
XLA Ops:
  0.6 68.2 %hyena_block.1 = (bf16[128,512]{1,0:T(8,128)(2,1)}, bf16[128,512]{1,0:T(8,128)(2,1)}, bf16[128,512]{1,0:T(8,128)(2,1)}, bf16[128,512]{1,0:T(8,128)(2,1)}, bf16[512,512]{1,0:T(8,128)(2,1)}) custom-call(bf16[128,512]{1,0:T(8,128)(2,1)} %q_ref.1, bf16[128,512]{1,0:T(8,128)(2,1)} %k_ref.1, bf16[128,512]{1,0:T(8,128)(2,1)} %v_ref.1, f32[16,512]{1,0:T(8,128)} %res_ref.1, ...), custom_call_target="tpu_custom_call" | custom-call | tf_op jit(solution)/shard_map/hyena_block/pallas_call | solution.py:510
  68.8 1.6 %copy.17 = bf16[128,512]{1,0:T(8,128)(2,1)} copy(bf16[128,512]{1,0:T(8,128)(2,1)} %get-tuple-element.10) | data formatting | bytes 262144
  70.4 1.6 %copy.18 = bf16[128,512]{1,0:T(8,128)(2,1)} copy(bf16[128,512]{1,0:T(8,128)(2,1)} %get-tuple-element.11) | data formatting | bytes 262144
  72.0 1.6 %copy.19 = bf16[128,512]{1,0:T(8,128)(2,1)} copy(bf16[128,512]{1,0:T(8,128)(2,1)} %get-tuple-element.12) | data formatting | bytes 262144
  73.5 1.6 %copy.20 = bf16[128,512]{1,0:T(8,128)(2,1)} copy(bf16[128,512]{1,0:T(8,128)(2,1)} %get-tuple-element.13) | data formatting | bytes 262144
  75.1 1.9 %copy.21 = bf16[512,512]{1,0:T(8,128)(2,1)} copy(bf16[512,512]{1,0:T(8,128)(2,1)} %get-tuple-element.14) | data formatting | bytes 1048576
where the time goes:
time: 78.2 us; the launch traced here: 77 us
  Pallas kernels  68.2 us (87%)
  local copies, waits for them, and re-layouts  8.14 us (10%)
    pallas_call x1, Pallas kernels, shards(): pl.pallas_call(functools.partial(body, X, Y, Z), out_shape=(small, small,...  68.2 us
    unnamed x5, local copies, waits for them, and re-layouts  8.14 us

commit v1 on v0

v1 whole, which is shorter than its diff:
```python
import functools
import math

import jax
import jax.numpy as jnp
import ml_dtypes
import numpy as np
from jax import lax
from jax.experimental import pallas as pl
from jax.experimental.pallas import tpu as pltpu
from jax.sharding import PartitionSpec as P

MESH = pl.DeviceIdType.MESH
F32 = jnp.float32
BF16 = jnp.bfloat16
LANES = 128


def body(
    X, Y, Z,
    q_in, k_in, v_in, res_in, dec_in, w_ref, cot_in, fold_in, unfold_in,
    mixed_ref, qg_ref, kg_ref, vg_ref, wg_ref,
    wv, cot_all, cot_t, gat, part, sib, rs_out, rs_in, states, row_states,
    q_ref, k_ref, v_ref, res_ref, dec_ref, fold, unfold, in_sem,
    src, cgr, conv, back, mix, taps, taps_hat, wacc, rates, weights, powers, starts,
    mixed_buf, qg_buf, kg_buf, vg_buf, wg_buf, out_sem,
    w_sem, ag_ss, ag_rs, cs_ss, cs_rs, aa_ss, aa_rs, fw_ss, fw_rs, ex_ss, ex_rs, st_ss, st_rs, ro_ss, ro_rs,
    g1_ss, g1_rs, g2_ss, g2_rs, sb_ss, sb_rs, rr_ss, rr_rs,
):
    N = X * Y
    R, C = q_in.shape
    M = dec_in.shape[0]
    T = R // 8
    G = C // LANES
    H = Z // 2
    c = lax.axis_index("context")
    j = lax.axis_index("tensor")
    z, r = j // 2, j % 2
    cx, cy = c // Y, c % Y
    other = z * 2 + 1 - r
    mine = (c, j)
    sibling = (c, other)
    zdev = [(c, ((z + 1) % Z) * 2 + r), (c, ((z + Z - 1) % Z) * 2 + r)]
    xdev = [(((cx + 1) % X) * Y + cy, j), (((cx + X - 1) % X) * Y + cy, j)]
    ydev = [(cx * Y + (cy + 1) % Y, j), (cx * Y + (cy + Y - 1) % Y, j)]

    def copy(source, target, send_sem, recv_sem, device):
        return pltpu.make_async_remote_copy(
            src_ref=source, dst_ref=target, send_sem=send_sem, recv_sem=recv_sem,
            device_id=device, device_id_type=MESH,
        )

    def lanes_of(g):
        return pl.ds(pl.multiple_of(g * LANES, LANES), LANES)

    barrier = pltpu.get_barrier_semaphore()
    for device in zdev + [sibling]:
        pl.semaphore_signal(barrier, inc=1, device_id=device, device_id_type=MESH)

    @pl.loop(0, N)
    def _(p):
        @pl.when(p != c)
        def _():
            pl.semaphore_signal(barrier, inc=1, device_id=(p, j), device_id_type=MESH)

    loads = (
        (k_in, k_ref), (v_in, v_ref), (dec_in, dec_ref), (cot_in, cot_all.at[j]), (res_in, res_ref),
        (fold_in, fold), (q_in, q_ref), (unfold_in, unfold),
    )

    def load(n):
        return pltpu.make_async_copy(*loads[n], in_sem.at[n])

    for n in range(len(loads)):
        load(n).start()

    def w_copy(n):
        return pltpu.make_async_copy(
            w_ref.at[:, pl.ds(pl.multiple_of(n * C, LANES), C)], wv.at[n], w_sem.at[n]
        )

    @pl.loop(0, 2 * Z)
    def _(n):
        w_copy(n).start()

    rows8 = lax.broadcasted_iota(jnp.int32, (8, LANES), 0).astype(F32)

    def spread_weights():
        load(4).wait()
        weight = res_ref[...] * jnp.sqrt(dec_ref[...])
        for m in range(M):
            weights[m] = jnp.broadcast_to(weight[m : m + 1], (8, C))

    def spread_rates():
        for m in range(M):
            rate = jnp.broadcast_to(dec_ref[pl.ds(m, 1), :], (8, C))
            rates[m] = rate
            powers[m] = jnp.exp(-8.0 * rate)

    def local_states(values, forward):
        way = 0 if forward else 1

        @pl.loop(0, G)
        def _(g):
            lanes = lanes_of(g)
            tiles = [values[pl.ds(8 * a, 8), lanes] for a in range(T)]
            if not forward:
                tiles = tiles[::-1]

            @pl.loop(0, M // 8)
            def _(eight):
                sums = []
                for inner in range(8):
                    m = eight * 8 + inner
                    step = powers[m, :, lanes]
                    total = tiles[0]
                    for tile in tiles[1:]:
                        total = total * step + tile
                    reach = 7.0 - rows8 if forward else rows8
                    total = total * jnp.exp(-rates[m, :, lanes] * reach)
                    sums.append(jnp.sum(total, axis=0, keepdims=True))
                modes = pl.ds(pl.multiple_of(eight * 8, 8), 8)
                states[way, cy, modes, lanes] = jnp.concatenate(sums, axis=0)

    def filter_taps():
        @pl.loop(0, G)
        def _(g):
            lanes = lanes_of(g)

            def add_mode(m, tiles):
                step = powers[m, :, lanes]
                term = weights[m, :, lanes] * jnp.exp(-rates[m, :, lanes] * rows8)
                new = []
                for a in range(T):
                    new.append(tiles[a] + term)
                    term = term * step
                return tuple(new)

            zero = jnp.zeros((8, LANES), F32)
            tiles = lax.fori_loop(0, M, add_mode, (zero,) * T, unroll=4)
            for a in range(T):
                taps[pl.ds(8 * a, 8), lanes] = tiles[a]

    width = min(C, 256)

    def halves(value):
        high = value.astype(BF16)
        return high, (value - high.astype(F32)).astype(BF16)

    def analyse(value):
        high, low = halves(value)
        return jnp.dot(fold[...], jnp.concatenate([high, high, low]), preferred_element_type=F32)

    def filter_spectrum():
        for lo in range(0, C, width):
            lanes = slice(lo, lo + width)
            taps_hat[:, lanes] = analyse(taps[:, lanes])

    def convolve(values, forward, out):
        for lo in range(0, C, width):
            lanes = slice(lo, lo + width)
            both = analyse(values[:, lanes])
            real, imag = both[:R], both[R:]
            tap_real, tap_imag = taps_hat[:R, lanes], taps_hat[R:, lanes]
            if forward:
                new_real = tap_real * real - tap_imag * imag
                new_imag = tap_real * imag + tap_imag * real
            else:
                new_real = tap_real * real + tap_imag * imag
                new_imag = tap_real * imag - tap_imag * real
            real_high, real_low = halves(new_real)
            imag_high, imag_low = halves(new_imag)
            out[:, lanes] = jnp.dot(
                unfold[...],
                jnp.concatenate([real_high, imag_high, real_high, imag_high, real_low, imag_low]),
                preferred_element_type=F32,
            )

    def carry_in(forward):
        way = 0 if forward else 1
        decay = jnp.exp(-float(R) * dec_ref[...])
        row_decay = jnp.exp(-float(R * Y) * dec_ref[...])

        def add_row(n, total):
            return total * row_decay + row_states[way, n if forward else X - 1 - n]

        def add_block(n, total):
            return total * decay + states[way, n if forward else Y - 1 - n]

        total = lax.fori_loop(0, cx if forward else X - 1 - cx, add_row, jnp.zeros((M, C), F32))
        total = lax.fori_loop(0, cy if forward else Y - 1 - cy, add_block, total)
        for m in range(M):
            starts[m] = weights[m] * total[m : m + 1]

    def add_carry(forward, out):
        @pl.loop(0, G)
        def _(g):
            lanes = lanes_of(g)

            def add_mode(m, tiles):
                rate, step = rates[m, :, lanes], powers[m, :, lanes]
                term = starts[m, :, lanes] * jnp.exp(-rate * ((rows8 + 1.0) if forward else (8.0 - rows8)))
                new = []
                for a in range(T):
                    new.append(tiles[a] + term)
                    term = term * step
                return tuple(new)

            order = list(range(T)) if forward else list(range(T))[::-1]
            tiles = lax.fori_loop(
                0, M, add_mode, tuple(out[pl.ds(8 * a, 8), lanes] for a in order), unroll=4
            )
            for n, a in enumerate(order):
                out[pl.ds(8 * a, 8), lanes] = tiles[n]

    def state_copy(way, y, sending):
        ref = states.at[way, cy if sending else y]
        sem = st_rs.at[way, cy if sending else y]
        return copy(ref, ref, st_ss.at[way, y], sem, (cx * Y + y, j))

    def row_copy(way, x, sending):
        ref = row_states.at[way, cx if sending else x]
        sem = ro_rs.at[way, cx if sending else x]
        return copy(ref, ref, ro_ss.at[way, x], sem, (x * Y + cy, j))

    def others(count, here, act):
        @pl.loop(0, count)
        def _(n):
            pl.when(n != here)(lambda: act(n))

    def later(way):
        return (cx + 1, X) if way == 0 else (0, cx)

    def sooner(way):
        return (0, cx) if way == 0 else (cx + 1, X)

    def send_states(way):
        others(Y, cy, lambda y: state_copy(way, y, True).start())

    def send_rows(way):
        others(Y, cy, lambda y: state_copy(way, y, False).wait_recv())
        decay = jnp.exp(-float(R) * dec_ref[...])
        order = range(Y) if way == 0 else range(Y)[::-1]
        total = states[way, order[0]]
        for y in order[1:]:
            total = total * decay + states[way, y]
        row_states[way, cx] = total

        @pl.loop(*later(way))
        def _(x):
            row_copy(way, x, True).start()

    def wait_rows(way):
        @pl.loop(*sooner(way))
        def _(x):
            row_copy(way, x, False).wait_recv()

    def drain_states(way):
        others(Y, cy, lambda y: state_copy(way, y, True).wait_send())

        @pl.loop(*later(way))
        def _(x):
            row_copy(way, x, True).wait_send()

    def piece(way, hop, last, size):
        if hop < last:
            return pl.ds(0, size)
        return pl.ds(way * (size // 2), size // 2)

    def ag_copy(way, hop, k, sending):
        away = hop - 1 if sending else hop
        owner = (z - away + Z) % Z if way == 0 else (z + away) % Z
        ref = cot_all.at[owner * 2 + r, pl.ds(k * (R // 2), R // 2)]
        return copy(ref, ref, ag_ss.at[way, hop - 1, k], ag_rs.at[way, hop - 1, k], zdev[way])

    def ag_pieces(hop):
        return [(way, k) for k in range(2) for way in range(2) if hop < H or way == k]

    def cs_copy(zz, sending):
        ref = cot_all.at[zz * 2 + (r if sending else 1 - r)]
        return copy(ref, ref, cs_ss.at[zz], cs_rs.at[zz], sibling)

    odd = z % 2
    own_rows = pl.ds(pl.multiple_of(odd * (R // 2), R // 2), R // 2)
    other_rows = pl.ds(pl.multiple_of((1 - odd) * (R // 2), R // 2), R // 2)

    def aa_copy(zz):
        owner = zz * 2 + r
        return copy(
            cot_all.at[owner, own_rows], cot_t.at[cx, cy, own_rows], aa_ss.at[zz], aa_rs.at[c], (owner, j)
        )

    def spread(zz):
        cs_copy(zz, True).start()

    def scatter(lo, hi):
        count = hi - lo

        @pl.loop(0, count)
        def _(n):
            zz = (z + Z + lo + (c // 2 + n) % count) % Z

            @pl.when(zz * 2 + r != c)
            def _():
                aa_copy(zz).start()

    def ag_start():
        for way, k in ag_pieces(1):
            ag_copy(way, 1, k, True).start()

    def ag_arrive(hop, half_at):
        for way, k in ag_pieces(hop):
            if k == half_at:
                ag_copy(way, hop, k, False).wait_recv()
                if (way, k) in ag_pieces(hop + 1) and hop < H:
                    ag_copy(way, hop + 1, k, True).start()
        if half_at == 1:
            spread((z + hop) % Z)
            if hop < H:
                spread((z - hop + Z) % Z)

    half = R // 2

    def g1_copy(part_at, way, hop, sending):
        size, last, devices, at = (X, X // 2, xdev, cx) if part_at == 0 else (Y, Y // 2, ydev, cy)
        away = hop - 1 if sending else hop
        owner = (at - away + size) % size if way == 0 else (at + away) % size
        low = part_at * half
        if hop == last:
            rows = pl.ds(low + way * (half // 2), half // 2)
        else:
            rows = pl.ds(low, half)
        ref = gat.at[owner, cy, rows] if part_at == 0 else gat.at[cx, owner, rows]
        return copy(ref, ref, g1_ss.at[part_at, way, hop - 1], g1_rs.at[part_at, way, hop - 1], devices[way])

    def g2_copy(part_at, way, hop, sending):
        size, last, devices, at, many = (
            (Y, Y // 2, ydev, cy, X) if part_at == 0 else (X, X // 2, xdev, cx, Y)
        )
        away = hop - 1 if sending else hop
        owner = (at - away + size) % size if way == 0 else (at + away) % size
        group = piece(way, hop, last, many)
        rows = pl.ds(part_at * half, half)
        ref = gat.at[group, owner, rows] if part_at == 0 else gat.at[owner, group, rows]
        return copy(ref, ref, g2_ss.at[part_at, way, hop - 1], g2_rs.at[part_at, way, hop - 1], devices[way])

    def hops_of(phase, part_at):
        return (X // 2, Y // 2)[part_at if phase == 1 else 1 - part_at]

    def gather_send(phase, hop):
        make = g1_copy if phase == 1 else g2_copy
        for part_at in range(2):
            if hop <= hops_of(phase, part_at):
                for way in range(2):
                    make(part_at, way, hop, True).start()

    def gather_wait(phase, hop):
        make = g1_copy if phase == 1 else g2_copy
        for part_at in range(2):
            if hop <= hops_of(phase, part_at):
                for way in range(2):
                    make(part_at, way, hop, False).wait_recv()

    def sb_copy(zz, sending):
        target = zz * 2 + (1 - r if sending else r)
        return copy(part.at[target], sib.at[zz], sb_ss.at[zz], sb_rs.at[zz], sibling)

    def project(lo, hi):
        @pl.loop(lo, hi)
        def _(o):
            hop = H - (o + 1) // 2
            zz = (z + Z + hop * (2 * (o % 2) - 1)) % Z
            gated = gat[cx, cy]
            for core in range(2):
                target = zz * 2 + ((1 - r) if core == 0 else r)
                part[target] = jnp.dot(
                    gated, wv[target], preferred_element_type=F32
                ).astype(BF16)
                if core == 0:
                    sb_copy(zz, True).start()

    halves_of = (pl.ds(0, half), pl.ds(half, half))

    def rr_copy(way, step, k):
        return copy(
            rs_out.at[way, step, halves_of[k]], rs_in.at[way, step, halves_of[k]],
            rr_ss.at[way, step, k], rr_rs.at[way, step, k], zdev[way],
        )

    def pair_sum(zz, k):
        return part[zz * 2 + r, halves_of[k]].astype(F32) + sib[zz, halves_of[k]].astype(F32)

    def reduce_target(way, step):
        away = H - step
        return (z + away) % Z if way == 0 else (z - away + Z) % Z

    def reduce_piece(way, step, k, arrived):
        total = pair_sum(reduce_target(way, step), k)
        if arrived:
            rr_copy(way, step - 1, k).wait_recv()
            total = total + rs_in[way, step - 1, halves_of[k]].astype(F32)
        rs_out[way, step, halves_of[k]] = total.astype(BF16)
        rr_copy(way, step, k).start()

    def reduce_first():
        sb_copy((z + H) % Z, False).wait_recv()
        for way in range(2):
            reduce_piece(way, 0, way, False)
        if H > 1:
            for way in range(2):
                sb_copy(reduce_target(way, 1), False).wait_recv()
                reduce_piece(way, 1, 1 - way, False)

    def reduce_second():
        if H > 1:
            for way in range(2):
                reduce_piece(way, 1, way, True)

    def reduce_step(step, k):
        if step < H:
            for way in range(2):
                if k == 0:
                    sb_copy(reduce_target(way, step), False).wait_recv()
                reduce_piece(way, step, k, True)

    def reduce_pieces():
        return [
            (way, step, k) for step in range(H) for way in range(2) for k in range(2)
            if step > 0 or k == way
        ]

    def reduce_last():
        sb_copy(z, False).wait_recv()
        for k in range(2):
            total = pair_sum(z, k)
            for way in range(2):
                if H > 1 or way == k:
                    rr_copy(way, H - 1, k).wait_recv()
                    total = total + rs_in[way, H - 1, halves_of[k]].astype(F32)
            mixed_buf[halves_of[k]] = total.astype(BF16)

    active = c % 2 == r

    def fw_copy(own, p):
        ref = cot_t.at[p // Y, p % Y, own_rows if own else other_rows]
        n = 0 if own else 1
        return copy(ref, ref, fw_ss.at[n, p], fw_rs.at[n, p], sibling)

    def ex_copy(way, p, sending):
        side = odd if sending else 1 - odd
        low = pl.multiple_of(side * (R // 2) + way * (R // 4), R // 4)
        ref = cot_t.at[p // Y, p % Y, pl.ds(low, R // 4)]
        return copy(ref, ref, ex_ss.at[way, p], ex_rs.at[way, p], zdev[way])

    def aa_arrived(p):
        ref = cot_t.at[p // Y, p % Y, own_rows]
        return copy(ref, ref, aa_ss.at[0], aa_rs.at[p], mine)

    def pass_one(p):
        aa_arrived(p).wait_recv()
        for way in range(2):
            ex_copy(way, p, True).start()
        fw_copy(True, p).start()

    def pass_on():
        pl.when(active)(lambda: others(N, c, pass_one))

    def hand_one(p):
        for way in range(2):
            ex_copy(way, p, False).wait_recv()
        fw_copy(False, p).start()

    def hand_over():
        pl.when(active)(lambda: others(N, c, hand_one))

    def handed_own():
        pl.when(jnp.logical_not(active))(
            lambda: others(N, c, lambda p: fw_copy(True, p).wait_recv())
        )
        cot_t[cx, cy] = cot_all[c]

    def handed_over():
        pl.when(jnp.logical_not(active))(
            lambda: others(N, c, lambda p: fw_copy(False, p).wait_recv())
        )

    def drain_one(p):
        for way in range(2):
            ex_copy(way, p, True).wait_send()
        fw_copy(True, p).wait_send()
        fw_copy(False, p).wait_send()

    def wait_weights():
        @pl.loop(0, 2 * Z)
        def _(n):
            w_copy(n).wait()

    def begin():
        for n in (0, 1, 2):
            load(n).wait()
        src[...] = k_ref[...].astype(F32) * v_ref[...].astype(F32)
        spread_rates()
        local_states(src, True)

    def first_sends():
        load(3).wait()
        ag_start()
        send_states(0)
        spread(z)

    def filter_spectrum_loaded():
        for n in (5, 6, 7):
            load(n).wait()
        filter_spectrum()

    def gate():
        carry_in(True)
        add_carry(True, conv)
        gat[cx, cy] = (q_ref[...].astype(F32) * conv[...]).astype(BF16)
        gather_send(1, 1)

    def multiply_back(distances, first=False):
        if not distances:
            return
        zs = [(z + Z + away) % Z for away in distances]
        blocks = [zz * 2 + core for zz in zs for core in range(2)]
        total = lax.dot_general(
            jnp.concatenate([cot_all[n] for n in blocks], axis=1),
            jnp.concatenate([wv[n] for n in blocks], axis=1),
            (((1,), (1,)), ((), ())), preferred_element_type=F32,
        )
        back[...] = total if first else back[...] + total

    def sibling_here(distances):
        for away in distances:
            cs_copy((z + Z + away) % Z, False).wait_recv()

    def back_states():
        qg_buf[...] = (back[...] * conv[...]).astype(BF16)
        put(0, qg_buf, qg_ref).start()
        cgr[...] = back[...] * q_ref[...].astype(F32)
        local_states(cgr, False)
        send_states(1)

    def key_value():
        carry_in(False)
        add_carry(False, mix)
        kg_buf[...] = (mix[...] * v_ref[...].astype(F32)).astype(BF16)
        put(1, kg_buf, kg_ref).start()
        vg_buf[...] = (mix[...] * k_ref[...].astype(F32)).astype(BF16)
        put(2, vg_buf, vg_ref).start()

    def mixed_done():
        reduce_last()
        put(3, mixed_buf, mixed_ref).start()

    def weight_product(rows, first):
        total = lax.dot_general(
            gat[:, :, rows].reshape(N * half, C), cot_t[:, :, rows].reshape(N * half, C),
            (((0,), (0,)), ((), ())), preferred_element_type=F32,
        )
        if first:
            wacc[...] = total
        else:
            wg_buf[...] = (wacc[...] + total).astype(BF16)
            put(4, wg_buf, wg_ref).start()

    def put(n, buffer, out):
        return pltpu.make_async_copy(buffer, out, out_sem.at[n])

    def drain():
        drain_states(0)
        drain_states(1)
        for way in range(2):
            for phase, make in ((1, g1_copy), (2, g2_copy)):
                for part_at in range(2):
                    for hop in range(1, hops_of(phase, part_at) + 1):
                        make(part_at, way, hop, True).wait_send()

        for hop in range(1, H + 1):
            for way, k in ag_pieces(hop):
                ag_copy(way, hop, k, True).wait_send()
        for way, step, k in reduce_pieces():
            rr_copy(way, step, k).wait_send()

        @pl.loop(0, Z)
        def _(zz):
            cs_copy(zz, True).wait_send()
            sb_copy(zz, True).wait_send()

            @pl.when(zz * 2 + r != c)
            def _():
                aa_copy(zz).wait_send()

        pl.when(active)(lambda: others(N, c, drain_one))
        buffers = ((qg_buf, qg_ref), (kg_buf, kg_ref), (vg_buf, vg_ref), (mixed_buf, mixed_ref), (wg_buf, wg_ref))
        for n, (buffer, out) in enumerate(buffers):
            put(n, buffer, out).wait()

    top = max(X // 2, Y // 2)

    def arrive(hop, k):
        if hop < H:
            ag_arrive(hop, k)

    def gather_on(phase, lo, last=False):
        for hop in range(lo, top + 1):
            gather_wait(phase, hop) if last else gather_send(phase, hop)

    assert H <= 4
    near = list(range(-min(2, H - 1), min(2, H - 1) + 1))
    far = [away for away in range(-H + 1, H + 1) if away not in near]
    def scatter_at(away):
        if away <= H:
            scatter(away, away + 1)
            if away < H:
                scatter(-away, -away + 1)

    def projects(lo, hi):
        return lambda: project(min(lo, Z), min(hi, Z))

    steps = [
        ("begin", begin),
        ("barrier", lambda: pl.semaphore_wait(barrier, N - 1 + 3)),
        ("first_sends", first_sends),
        ("weights", spread_weights),
        ("taps", filter_taps),
        ("spectrum", filter_spectrum_loaded),
        ("send_rows", lambda: send_rows(0)),
        ("arrive1a", lambda: arrive(1, 0)),
        ("convolve", lambda: convolve(src, True, conv)),
        ("arrive1b", lambda: arrive(1, 1)),
        ("wait_rows", lambda: wait_rows(0)),
        ("gate", gate),
        ("scatter1", lambda: scatter(-min(1, H - 1), min(1, H - 1) + 1)),
        ("arrive2a", lambda: arrive(2, 0)),
        ("wait_weights", wait_weights),
        ("project_1", projects(0, 3)),
        ("arrive2b", lambda: arrive(2, 1)),
        ("reduce_first", reduce_first),
        ("scatter2", lambda: scatter_at(2) if H > 2 else None),
        ("project_2", projects(3, 5)),
        ("arrive3a", lambda: arrive(3, 0)),
        ("gather1_wait1", lambda: gather_wait(1, 1)),
        ("gather1_send2", lambda: gather_on(1, 2)),
        ("project_3", projects(5, Z)),
        ("arrive3b", lambda: arrive(3, 1)),
        ("reduce_second", reduce_second),
        ("scatter3", lambda: scatter_at(3) if H > 3 else None),
        ("gather1_wait2", lambda: gather_on(1, 2, True)),
        ("gather2_send1", lambda: gather_send(2, 1)),
        ("sibling_near", lambda: sibling_here(near)),
        ("back_near", lambda: multiply_back(near, True)),
        ("arrive_last", lambda: (ag_arrive(H, 0), ag_arrive(H, 1))),
        ("scatter_last", lambda: scatter_at(H)),
        ("reduce2a", lambda: reduce_step(2, 0)),
        ("sibling_far", lambda: sibling_here(far)),
        ("back_far", lambda: multiply_back(far)),
        ("reduce2b", lambda: reduce_step(2, 1)),
        ("back_states", back_states),
        ("correlate", lambda: convolve(cgr, False, mix)),
        ("pass_on", pass_on),
        ("reduce3a", lambda: reduce_step(3, 0)),
        ("gather2_wait1", lambda: gather_wait(2, 1)),
        ("gather2_send2", lambda: gather_on(2, 2)),
        ("reduce3b", lambda: reduce_step(3, 1)),
        ("send_back_rows", lambda: send_rows(1)),
        ("hand_over", hand_over),
        ("wait_back_rows", lambda: wait_rows(1)),
        ("key_value", key_value),
        ("handed_own", handed_own),
        ("gather2_wait2", lambda: gather_on(2, 2, True)),
        ("weight_own", lambda: weight_product(own_rows, True)),
        ("mixed_done", mixed_done),
        ("handed_over", handed_over),
        ("weight_other", lambda: weight_product(other_rows, False)),
        ("drain", drain),
    ]
    for name, step in steps:
        step()


def transforms(R):
    angle = np.pi / (2 * R) * (np.outer(2 * np.arange(R) + 1, np.arange(R)) % (4 * R))
    there = np.concatenate([np.cos(angle), -np.sin(angle)])
    result = []
    for table in (there, there.T / R):
        high = table.astype(np.float32).astype(ml_dtypes.bfloat16)
        low = (table - high.astype(np.float64)).astype(ml_dtypes.bfloat16)
        result.append(jnp.asarray(np.concatenate([high, low, high], axis=1)))
    return result


def finish(*refs):
    count = len(refs) // 3
    given, made, held = refs[:count], refs[count : 2 * count], refs[2 * count : 3 * count]
    in_sem, out_sem = refs[3 * count :]
    ins = [pltpu.make_async_copy(a, b, in_sem.at[n]) for n, (a, b) in enumerate(zip(given, held))]
    outs = [pltpu.make_async_copy(a, b, out_sem.at[n]) for n, (a, b) in enumerate(zip(held, made))]
    for one in ins:
        one.start()
    for one, other in zip(ins, outs):
        one.wait()
        other.start()
    for one in outs:
        one.wait()


def solution(mesh):
    N = mesh.shape["context"]
    X = math.isqrt(N)
    Y = N // X
    Z = mesh.shape["tensor"] // 2
    H = Z // 2

    def shards(query_rows, key_rows, value_rows, residue, decay_rate, out_weight, cotangent):
        R, C = query_rows.shape
        M = residue.shape[0]
        small = jax.ShapeDtypeStruct((R, C), BF16)
        dma = pltpu.SemaphoreType.DMA
        top = max(X // 2, Y // 2)
        anywhere = pl.BlockSpec(memory_space=pl.ANY)
        results = (small, small, small, small, jax.ShapeDtypeStruct((C, C), BF16))
        made = pl.pallas_call(
            functools.partial(body, X, Y, Z),
            out_shape=results,
            in_specs=[anywhere] * 9,
            out_specs=(anywhere,) * 5,
            scratch_shapes=[
                pltpu.VMEM((2 * Z, C, C), BF16),
                pltpu.VMEM((2 * Z, R, C), BF16),
                pltpu.VMEM((X, Y, R, C), BF16),
                pltpu.VMEM((X, Y, R, C), BF16),
                pltpu.VMEM((2 * Z, R, C), BF16),
                pltpu.VMEM((Z, R, C), BF16),
                pltpu.VMEM((2, H, R, C), BF16),
                pltpu.VMEM((2, H, R, C), BF16),
                pltpu.VMEM((2, Y, M, C), F32),
                pltpu.VMEM((2, X, M, C), F32),
                pltpu.VMEM((R, C), BF16),
                pltpu.VMEM((R, C), BF16),
                pltpu.VMEM((R, C), BF16),
                pltpu.VMEM((M, C), F32),
                pltpu.VMEM((M, C), F32),
                pltpu.VMEM((2 * R, 3 * R), BF16),
                pltpu.VMEM((R, 6 * R), BF16),
                dma((8,)),
                pltpu.VMEM((R, C), F32),
                pltpu.VMEM((R, C), F32),
                pltpu.VMEM((R, C), F32),
                pltpu.VMEM((R, C), F32),
                pltpu.VMEM((R, C), F32),
                pltpu.VMEM((R, C), F32),
                pltpu.VMEM((2 * R, C), F32),
                pltpu.VMEM((C, C), F32),
                pltpu.VMEM((M, 8, C), F32),
                pltpu.VMEM((M, 8, C), F32),
                pltpu.VMEM((M, 8, C), F32),
                pltpu.VMEM((M, 8, C), F32),
                pltpu.VMEM((R, C), BF16),
                pltpu.VMEM((R, C), BF16),
                pltpu.VMEM((R, C), BF16),
                pltpu.VMEM((R, C), BF16),
                pltpu.VMEM((C, C), BF16),
                dma((5,)),
                dma((2 * Z,)),
                dma((2, H, 2)),
                dma((2, H, 2)),
                dma((Z,)),
                dma((Z,)),
                dma((Z,)),
                dma((N,)),
                dma((2, N)),
                dma((2, N)),
                dma((2, N)),
                dma((2, N)),
                dma((2, Y)),
                dma((2, Y)),
                dma((2, X)),
                dma((2, X)),
                dma((2, 2, top)),
                dma((2, 2, top)),
                dma((2, 2, top)),
                dma((2, 2, top)),
                dma((Z,)),
                dma((Z,)),
                dma((2, H, 2)),
                dma((2, H, 2)),
            ],
            compiler_params=pltpu.CompilerParams(
                collective_id=0, has_side_effects=True, vmem_limit_bytes=56 * 1024 * 1024
            ),
            name="hyena_block",
        )(query_rows, key_rows, value_rows, residue, decay_rate, out_weight, cotangent, *transforms(R))
        return pl.pallas_call(
            finish,
            out_shape=results,
            in_specs=[anywhere] * 5,
            out_specs=(anywhere,) * 5,
            scratch_shapes=[pltpu.VMEM(one.shape, BF16) for one in results] + [dma((5,)), dma((5,))],
            compiler_params=pltpu.CompilerParams(vmem_limit_bytes=56 * 1024 * 1024),
            name="hand_out",
        )(*made)

    placed = (
        P("context", "tensor"),
        P("context", "tensor"),
        P("context", "tensor"),
        P(None, "tensor"),
        P(None, "tensor"),
        P("tensor", None),
        P("context", "tensor"),
    )
    return jax.shard_map(
        shards,
        mesh=mesh,
        in_specs=placed,
        out_specs=(
            P("context", "tensor"),
            P("context", "tensor"),
            P("context", "tensor"),
            P("context", "tensor"),
            P("tensor", "context"),
        ),
        check_vma=False,
    )
```

time: 78.2 us -> 57.2 us (0.73)
  the two profiles are of different devices: /device:TPU:64 before, /device:TPU:96 now
where the time goes in v1:
time: 57.2 us; the launch traced here: 57.1 us
  Pallas kernels  56.4 us (99%)
  between operations  0.64 us (1%)
    pallas_call x1, Pallas kernels, shards(): pl.pallas_call(functools.partial(body, X, Y, Z), out_shape=results, in_sp...  54.2 us
    pallas_call x1, Pallas kernels, shards(): pl.pallas_call(finish, out_shape=results, in_specs=[anywhere] * 5, out_sp...  2.19 us

profile of v1, /device:TPU:96, one launch (start us, length us, event | category | flops | bytes accessed | tf_op | source)
XLA Modules:
  0.0 57.1 jit_solution(11235836218193376584)
XLA Ops:
  0.6 54.2 %hyena_block.1 = (bf16[128,512]{1,0:T(8,128)(2,1)}, bf16[128,512]{1,0:T(8,128)(2,1)}, bf16[128,512]{1,0:T(8,128)(2,1)}, bf16[128,512]{1,0:T(8,128)(2,1)}, bf16[512,512]{1,0:T(8,128)(2,1)}) custom-call(bf16[128,512]{1,0:T(8,128)(2,1)} %q_in.1, bf16[128,512]{1,0:T(8,128)(2,1)} %k_in.1, bf16[128,512]{1,0:T(8,128)(2,1)} %v_in.1, f32[16,512]{1,0:T(8,128)} %res_in.1, ...), custom_call_target="tpu_custom_call" | custom-call | tf_op jit(solution)/shard_map/hyena_block/pallas_call | solution.py:724
  54.9 2.2 %hand_out.1 = (bf16[128,512]{1,0:T(8,128)(2,1)}, bf16[128,512]{1,0:T(8,128)(2,1)}, bf16[128,512]{1,0:T(8,128)(2,1)}, bf16[128,512]{1,0:T(8,128)(2,1)}, bf16[512,512]{1,0:T(8,128)(2,1)}) custom-call(bf16[128,512]{1,0:T(8,128)(2,1)} %get-tuple-element.10.refs_0_, bf16[128,512]{1,0:T(8,128)(2,1)} %get-tuple-element.11.refs_1_, ...), custom_call_target="tpu_custom_call" | custom-call | tf_op jit(solution)/shard_map/hand_out/pallas_call | solution.py:795

commit v2 on v1

--- a/solution.py
+++ b/solution.py
@@ -23,9 +23,8 @@
     wv, cot_all, cot_t, gat, part, sib, rs_out, rs_in, states, row_states,
     q_ref, k_ref, v_ref, res_ref, dec_ref, fold, unfold, in_sem,
     src, cgr, conv, back, mix, taps, taps_hat, wacc, rates, weights, powers, starts,
-    mixed_buf, qg_buf, kg_buf, vg_buf, wg_buf, out_sem,
     w_sem, ag_ss, ag_rs, cs_ss, cs_rs, aa_ss, aa_rs, fw_ss, fw_rs, ex_ss, ex_rs, st_ss, st_rs, ro_ss, ro_rs,
-    g1_ss, g1_rs, g2_ss, g2_rs, sb_ss, sb_rs, rr_ss, rr_rs,
+    ga_ss, g1_rs, g2_rs, sb_ss, sb_rs, rr_ss, rr_rs,
 ):
     N = X * Y
     R, C = q_in.shape
@@ -50,6 +49,12 @@
             device_id=device, device_id_type=MESH,
         )
 
+    def arrived(sem, ref):
+        copy(ref, ref, sem, sem, mine).wait_recv()
+
+    def left(sem, ref):
+        copy(ref, ref, sem, sem, mine).wait_send()
+
     def lanes_of(g):
         return pl.ds(pl.multiple_of(g * LANES, LANES), LANES)
 
@@ -76,7 +81,7 @@
 
     def w_copy(n):
         return pltpu.make_async_copy(
-            w_ref.at[:, pl.ds(pl.multiple_of(n * C, LANES), C)], wv.at[n], w_sem.at[n]
+            w_ref.at[:, pl.ds(pl.multiple_of(n * C, LANES), C)], wv.at[n], w_sem.at[0]
         )
 
     @pl.loop(0, 2 * Z)
@@ -215,30 +220,24 @@
 
     def state_copy(way, y, sending):
         ref = states.at[way, cy if sending else y]
-        sem = st_rs.at[way, cy if sending else y]
-        return copy(ref, ref, st_ss.at[way, y], sem, (cx * Y + y, j))
+        sem = st_rs.at[way]
+        return copy(ref, ref, st_ss.at[way], sem, (cx * Y + y, j))
 
     def row_copy(way, x, sending):
         ref = row_states.at[way, cx if sending else x]
-        sem = ro_rs.at[way, cx if sending else x]
-        return copy(ref, ref, ro_ss.at[way, x], sem, (x * Y + cy, j))
+        sem = ro_rs.at[way]
+        return copy(ref, ref, ro_ss.at[way], sem, (x * Y + cy, j))
 
     def others(count, here, act):
         @pl.loop(0, count)
         def _(n):
             pl.when(n != here)(lambda: act(n))
 
-    def later(way):
-        return (cx + 1, X) if way == 0 else (0, cx)
-
-    def sooner(way):
-        return (0, cx) if way == 0 else (cx + 1, X)
-
     def send_states(way):
         others(Y, cy, lambda y: state_copy(way, y, True).start())
 
     def send_rows(way):
-        others(Y, cy, lambda y: state_copy(way, y, False).wait_recv())
+        arrived(st_rs.at[way], states.at[way, pl.ds(0, Y - 1)])
         decay = jnp.exp(-float(R) * dec_ref[...])
         order = range(Y) if way == 0 else range(Y)[::-1]
         total = states[way, order[0]]
@@ -246,21 +245,17 @@
             total = total * decay + states[way, y]
         row_states[way, cx] = total
 
-        @pl.loop(*later(way))
-        def _(x):
-            row_copy(way, x, True).start()
+        others(X, cx, lambda x: row_copy(way, x, True).start())
 
     def wait_rows(way):
-        @pl.loop(*sooner(way))
-        def _(x):
-            row_copy(way, x, False).wait_recv()
+        arrived(ro_rs.at[way], row_states.at[way, pl.ds(0, X - 1)])
 
     def drain_states(way):
-        others(Y, cy, lambda y: state_copy(way, y, True).wait_send())
-
-        @pl.loop(*later(way))
-        def _(x):
-            row_copy(way, x, True).wait_send()
+        left(st_ss.at[way], states.at[way, pl.ds(0, Y - 1)])
+        left(ro_ss.at[way], row_states.at[way, pl.ds(0, X - 1)])
+
+    near = list(range(-min(2, H - 1), min(2, H - 1) + 1))
+    far = [away for away in range(-H + 1, H + 1) if away not in near]
 
     def piece(way, hop, last, size):
         if hop < last:
@@ -271,14 +266,18 @@
         away = hop - 1 if sending else hop
         owner = (z - away + Z) % Z if way == 0 else (z + away) % Z
         ref = cot_all.at[owner * 2 + r, pl.ds(k * (R // 2), R // 2)]
-        return copy(ref, ref, ag_ss.at[way, hop - 1, k], ag_rs.at[way, hop - 1, k], zdev[way])
+        return copy(ref, ref, ag_ss.at[0], ag_rs.at[way, hop - 1, k], zdev[way])
 
     def ag_pieces(hop):
         return [(way, k) for k in range(2) for way in range(2) if hop < H or way == k]
 
-    def cs_copy(zz, sending):
-        ref = cot_all.at[zz * 2 + (r if sending else 1 - r)]
-        return copy(ref, ref, cs_ss.at[zz], cs_rs.at[zz], sibling)
+    def spread(away):
+        ref = cot_all.at[(z + Z + away) % Z * 2 + r]
+        group = 0 if away in near else 1
+        copy(ref, ref, cs_ss.at[0], cs_rs.at[group], sibling).start()
+
+    def sibling_here(group):
+        arrived(cs_rs.at[group], cot_all.at[pl.ds(0, len((near, far)[group]))])
 
     odd = z % 2
     own_rows = pl.ds(pl.multiple_of(odd * (R // 2), R // 2), R // 2)
@@ -287,11 +286,8 @@
     def aa_copy(zz):
         owner = zz * 2 + r
         return copy(
-            cot_all.at[owner, own_rows], cot_t.at[cx, cy, own_rows], aa_ss.at[zz], aa_rs.at[c], (owner, j)
+            cot_all.at[owner, own_rows], cot_t.at[c, own_rows], aa_ss.at[0], aa_rs.at[cx], (owner, j)
         )
-
-    def spread(zz):
-        cs_copy(zz, True).start()
 
     def scatter(lo, hi):
         count = hi - lo
@@ -315,9 +311,9 @@
                 if (way, k) in ag_pieces(hop + 1) and hop < H:
                     ag_copy(way, hop + 1, k, True).start()
         if half_at == 1:
-            spread((z + hop) % Z)
+            spread(hop)
             if hop < H:
-                spread((z - hop + Z) % Z)
+                spread(-hop)
 
     half = R // 2
 
@@ -331,7 +327,7 @@
         else:
             rows = pl.ds(low, half)
         ref = gat.at[owner, cy, rows] if part_at == 0 else gat.at[cx, owner, rows]
-        return copy(ref, ref, g1_ss.at[part_at, way, hop - 1], g1_rs.at[part_at, way, hop - 1], devices[way])
+        return copy(ref, ref, ga_ss.at[0], g1_rs.at[hop - 1], devices[way])
 
     def g2_copy(part_at, way, hop, sending):
         size, last, devices, at, many = (
@@ -342,7 +338,7 @@
         group = piece(way, hop, last, many)
         rows = pl.ds(part_at * half, half)
         ref = gat.at[group, owner, rows] if part_at == 0 else gat.at[owner, group, rows]
-        return copy(ref, ref, g2_ss.at[part_at, way, hop - 1], g2_rs.at[part_at, way, hop - 1], devices[way])
+        return copy(ref, ref, ga_ss.at[0], g2_rs.at[hop - 1], devices[way])
 
     def hops_of(phase, part_at):
         return (X // 2, Y // 2)[part_at if phase == 1 else 1 - part_at]
@@ -355,15 +351,15 @@
                     make(part_at, way, hop, True).start()
 
     def gather_wait(phase, hop):
-        make = g1_copy if phase == 1 else g2_copy
-        for part_at in range(2):
-            if hop <= hops_of(phase, part_at):
-                for way in range(2):
-                    make(part_at, way, hop, False).wait_recv()
+        count = 2 if hop < X // 2 else 1
+        if phase == 1:
+            arrived(g1_rs.at[hop - 1], gat.at[0, pl.ds(0, count)])
+        else:
+            arrived(g2_rs.at[hop - 1], gat.at[pl.ds(0, count)])
 
     def sb_copy(zz, sending):
         target = zz * 2 + (1 - r if sending else r)
-        return copy(part.at[target], sib.at[zz], sb_ss.at[zz], sb_rs.at[zz], sibling)
+        return copy(part.at[target], sib.at[zz], sb_ss.at[0], sb_rs.at[zz], sibling)
 
     def project(lo, hi):
         @pl.loop(lo, hi)
@@ -384,7 +380,7 @@
     def rr_copy(way, step, k):
         return copy(
             rs_out.at[way, step, halves_of[k]], rs_in.at[way, step, halves_of[k]],
-            rr_ss.at[way, step, k], rr_rs.at[way, step, k], zdev[way],
+            rr_ss.at[0], rr_rs.at[way, step, k], zdev[way],
         )
 
     def pair_sum(zz, k):
@@ -423,12 +419,6 @@
                     sb_copy(reduce_target(way, step), False).wait_recv()
                 reduce_piece(way, step, k, True)
 
-    def reduce_pieces():
-        return [
-            (way, step, k) for step in range(H) for way in range(2) for k in range(2)
-            if step > 0 or k == way
-        ]
-
     def reduce_last():
         sb_copy(z, False).wait_recv()
         for k in range(2):
@@ -437,63 +427,68 @@
                 if H > 1 or way == k:
                     rr_copy(way, H - 1, k).wait_recv()
                     total = total + rs_in[way, H - 1, halves_of[k]].astype(F32)
-            mixed_buf[halves_of[k]] = total.astype(BF16)
+            mixed_ref[halves_of[k]] = total.astype(BF16)
 
     active = c % 2 == r
 
-    def fw_copy(own, p):
-        ref = cot_t.at[p // Y, p % Y, own_rows if own else other_rows]
-        n = 0 if own else 1
-        return copy(ref, ref, fw_ss.at[n, p], fw_rs.at[n, p], sibling)
-
-    def ex_copy(way, p, sending):
+    def fw_copy(own, n):
+        ref = cot_t.at[pl.ds(n * Y, Y), own_rows if own else other_rows]
+        return copy(ref, ref, fw_ss.at[0], fw_rs.at[0 if own else 1], sibling)
+
+    def ex_copy(way, n, sending):
         side = odd if sending else 1 - odd
         low = pl.multiple_of(side * (R // 2) + way * (R // 4), R // 4)
-        ref = cot_t.at[p // Y, p % Y, pl.ds(low, R // 4)]
-        return copy(ref, ref, ex_ss.at[way, p], ex_rs.at[way, p], zdev[way])
-
-    def aa_arrived(p):
-        ref = cot_t.at[p // Y, p % Y, own_rows]
-        return copy(ref, ref, aa_ss.at[0], aa_rs.at[p], mine)
-
-    def pass_one(p):
-        aa_arrived(p).wait_recv()
+        ref = cot_t.at[pl.ds(n * Y, Y), pl.ds(low, R // 4)]
+        return copy(ref, ref, ex_ss.at[0], ex_rs.at[way, n], zdev[way])
+
+    def group_arrived(n):
+        def some(count):
+            return lambda: arrived(aa_rs.at[n], cot_t.at[pl.ds(0, count), pl.ds(0, R // 2)])
+
+        pl.when(n == cx)(some(Y - 1))
+        pl.when(n != cx)(some(Y))
+
+    def pass_group(n):
+        group_arrived(n)
         for way in range(2):
-            ex_copy(way, p, True).start()
-        fw_copy(True, p).start()
-
-    def pass_on():
-        pl.when(active)(lambda: others(N, c, pass_one))
-
-    def hand_one(p):
+            ex_copy(way, n, True).start()
+        fw_copy(True, n).start()
+
+    reach = (z - c // 2 + Z) % Z
+
+    def pass_on(*distances):
+        chosen = [reach == away % Z for away in set(distances) | {-away for away in distances}]
+
+        @pl.when(jnp.logical_and(active, functools.reduce(jnp.logical_or, chosen)))
+        def _():
+            cot_t[c, own_rows] = cot_all[c, own_rows]
+            pl.loop(0, X)(pass_group)
+
+    def hand_group(n):
         for way in range(2):
-            ex_copy(way, p, False).wait_recv()
-        fw_copy(False, p).start()
+            ex_copy(way, n, False).wait_recv()
+        fw_copy(False, n).start()
 
     def hand_over():
-        pl.when(active)(lambda: others(N, c, hand_one))
-
-    def handed_own():
-        pl.when(jnp.logical_not(active))(
-            lambda: others(N, c, lambda p: fw_copy(True, p).wait_recv())
-        )
-        cot_t[cx, cy] = cot_all[c]
-
-    def handed_over():
-        pl.when(jnp.logical_not(active))(
-            lambda: others(N, c, lambda p: fw_copy(False, p).wait_recv())
-        )
-
-    def drain_one(p):
-        for way in range(2):
-            ex_copy(way, p, True).wait_send()
-        fw_copy(True, p).wait_send()
-        fw_copy(False, p).wait_send()
+        pl.when(active)(lambda: pl.loop(0, X)(hand_group))
+
+    def handed(own):
+        rows = pl.ds(0, R // 2)
+        pl.when(jnp.logical_not(active))(lambda: arrived(fw_rs.at[0 if own else 1], cot_t.at[:, rows]))
+
+    def drain_passed():
+        @pl.when(active)
+        def _():
+            left(ex_ss.at[0], cot_t.at[:, pl.ds(0, R // 2)])
+            left(fw_ss.at[0], cot_t)
+            left(aa_ss.at[0], cot_t.at[pl.ds(0, Z - 1), pl.ds(0, R // 2)])
+
+        @pl.when(jnp.logical_not(active))
+        def _():
+            left(aa_ss.at[0], cot_t.at[pl.ds(0, Z), pl.ds(0, R // 2)])
 
     def wait_weights():
-        @pl.loop(0, 2 * Z)
-        def _(n):
-            w_copy(n).wait()
+        pltpu.make_async_copy(wv, wv, w_sem.at[0]).wait()
 
     def begin():
         for n in (0, 1, 2):
@@ -504,9 +499,9 @@
 
     def first_sends():
         load(3).wait()
+        send_states(0)
         ag_start()
-        send_states(0)
-        spread(z)
+        spread(0)
 
     def filter_spectrum_loaded():
         for n in (5, 6, 7):
@@ -519,11 +514,11 @@
         gat[cx, cy] = (q_ref[...].astype(F32) * conv[...]).astype(BF16)
         gather_send(1, 1)
 
-    def multiply_back(distances, first=False):
+    def multiply_back(distances, cores, first=False):
         if not distances:
             return
         zs = [(z + Z + away) % Z for away in distances]
-        blocks = [zz * 2 + core for zz in zs for core in range(2)]
+        blocks = [zz * 2 + core for zz in zs for core in cores]
         total = lax.dot_general(
             jnp.concatenate([cot_all[n] for n in blocks], axis=1),
             jnp.concatenate([wv[n] for n in blocks], axis=1),
@@ -531,13 +526,8 @@
         )
         back[...] = total if first else back[...] + total
 
-    def sibling_here(distances):
-        for away in distances:
-            cs_copy((z + Z + away) % Z, False).wait_recv()
-
     def back_states():
-        qg_buf[...] = (back[...] * conv[...]).astype(BF16)
-        put(0, qg_buf, qg_ref).start()
+        qg_ref[...] = (back[...] * conv[...]).astype(BF16)
         cgr[...] = back[...] * q_ref[...].astype(F32)
         local_states(cgr, False)
         send_states(1)
@@ -545,57 +535,31 @@
     def key_value():
         carry_in(False)
         add_carry(False, mix)
-        kg_buf[...] = (mix[...] * v_ref[...].astype(F32)).astype(BF16)
-        put(1, kg_buf, kg_ref).start()
-        vg_buf[...] = (mix[...] * k_ref[...].astype(F32)).astype(BF16)
-        put(2, vg_buf, vg_ref).start()
+        kg_ref[...] = (mix[...] * v_ref[...].astype(F32)).astype(BF16)
+        vg_ref[...] = (mix[...] * k_ref[...].astype(F32)).astype(BF16)
 
     def mixed_done():
         reduce_last()
-        put(3, mixed_buf, mixed_ref).start()
 
     def weight_product(rows, first):
         total = lax.dot_general(
-            gat[:, :, rows].reshape(N * half, C), cot_t[:, :, rows].reshape(N * half, C),
+            gat[:, :, rows].reshape(N * half, C), cot_t[:, rows].reshape(N * half, C),
             (((0,), (0,)), ((), ())), preferred_element_type=F32,
         )
         if first:
             wacc[...] = total
         else:
-            wg_buf[...] = (wacc[...] + total).astype(BF16)
-            put(4, wg_buf, wg_ref).start()
-
-    def put(n, buffer, out):
-        return pltpu.make_async_copy(buffer, out, out_sem.at[n])
+            wg_ref[...] = (wacc[...] + total).astype(BF16)
 
     def drain():
         drain_states(0)
         drain_states(1)
-        for way in range(2):
-            for phase, make in ((1, g1_copy), (2, g2_copy)):
-                for part_at in range(2):
-                    for hop in range(1, hops_of(phase, part_at) + 1):
-                        make(part_at, way, hop, True).wait_send()
-
-        for hop in range(1, H + 1):
-            for way, k in ag_pieces(hop):
-                ag_copy(way, hop, k, True).wait_send()
-        for way, step, k in reduce_pieces():
-            rr_copy(way, step, k).wait_send()
-
-        @pl.loop(0, Z)
-        def _(zz):
-            cs_copy(zz, True).wait_send()
-            sb_copy(zz, True).wait_send()
-
-            @pl.when(zz * 2 + r != c)
-            def _():
-                aa_copy(zz).wait_send()
-
-        pl.when(active)(lambda: others(N, c, drain_one))
-        buffers = ((qg_buf, qg_ref), (kg_buf, kg_ref), (vg_buf, vg_ref), (mixed_buf, mixed_ref), (wg_buf, wg_ref))
-        for n, (buffer, out) in enumerate(buffers):
-            put(n, buffer, out).wait()
+        left(ag_ss.at[0], cot_all.at[pl.ds(0, Z - 1)])
+        left(cs_ss.at[0], cot_all.at[pl.ds(0, Z)])
+        left(sb_ss.at[0], sib)
+        left(rr_ss.at[0], cot_all.at[pl.ds(0, Z - 1)])
+        left(ga_ss.at[0], cot_all.at[pl.ds(0, N - 1)])
+        drain_passed()
 
     top = max(X // 2, Y // 2)
 
@@ -607,9 +571,7 @@
         for hop in range(lo, top + 1):
             gather_wait(phase, hop) if last else gather_send(phase, hop)
 
-    assert H <= 4
-    near = list(range(-min(2, H - 1), min(2, H - 1) + 1))
-    far = [away for away in range(-H + 1, H + 1) if away not in near]
+    assert H <= 4 and X == Y and N == 2 * Z
     def scatter_at(away):
         if away <= H:
             scatter(away, away + 1)
@@ -619,6 +581,7 @@
     def projects(lo, hi):
         return lambda: project(min(lo, Z), min(hi, Z))
 
+    same, both = (r,), (0, 1)
     steps = [
         ("begin", begin),
         ("barrier", lambda: pl.semaphore_wait(barrier, N - 1 + 3)),
@@ -632,47 +595,52 @@
         ("arrive1b", lambda: arrive(1, 1)),
         ("wait_rows", lambda: wait_rows(0)),
         ("gate", gate),
-        ("scatter1", lambda: scatter(-min(1, H - 1), min(1, H - 1) + 1)),
+        ("scatter01", lambda: scatter(-min(1, H - 1), min(1, H - 1) + 1)),
         ("arrive2a", lambda: arrive(2, 0)),
         ("wait_weights", wait_weights),
         ("project_1", projects(0, 3)),
         ("arrive2b", lambda: arrive(2, 1)),
-        ("reduce_first", reduce_first),
         ("scatter2", lambda: scatter_at(2) if H > 2 else None),
         ("project_2", projects(3, 5)),
         ("arrive3a", lambda: arrive(3, 0)),
+        ("project_3", projects(5, Z)),
+        ("arrive3b", lambda: arrive(3, 1)),
+        ("reduce_first", reduce_first),
+        ("scatter3", lambda: scatter_at(3) if H > 3 else None),
         ("gather1_wait1", lambda: gather_wait(1, 1)),
         ("gather1_send2", lambda: gather_on(1, 2)),
-        ("project_3", projects(5, Z)),
-        ("arrive3b", lambda: arrive(3, 1)),
+        ("sibling_near", lambda: sibling_here(0)),
+        ("back_near", lambda: multiply_back(near, both, True)),
+        ("pass_0", lambda: pass_on(0)),
+        ("arrive_last", lambda: (ag_arrive(H, 0), ag_arrive(H, 1))),
+        ("scatter_last", lambda: scatter_at(H)),
         ("reduce_second", reduce_second),
-        ("scatter3", lambda: scatter_at(3) if H > 3 else None),
+        ("back_far_same", lambda: multiply_back(far, same)),
+        ("pass_1", lambda: pass_on(1) if H > 1 else None),
         ("gather1_wait2", lambda: gather_on(1, 2, True)),
         ("gather2_send1", lambda: gather_send(2, 1)),
-        ("sibling_near", lambda: sibling_here(near)),
-        ("back_near", lambda: multiply_back(near, True)),
-        ("arrive_last", lambda: (ag_arrive(H, 0), ag_arrive(H, 1))),
-        ("scatter_last", lambda: scatter_at(H)),
+        ("pass_2", lambda: pass_on(2) if H > 2 else None),
+        ("sibling_far", lambda: sibling_here(1)),
+        ("back_far_other", lambda: multiply_back(far, (1 - r,))),
+        ("back_states", back_states),
         ("reduce2a", lambda: reduce_step(2, 0)),
-        ("sibling_far", lambda: sibling_here(far)),
-        ("back_far", lambda: multiply_back(far)),
+        ("correlate", lambda: convolve(cgr, False, mix)),
         ("reduce2b", lambda: reduce_step(2, 1)),
-        ("back_states", back_states),
-        ("correlate", lambda: convolve(cgr, False, mix)),
-        ("pass_on", pass_on),
-        ("reduce3a", lambda: reduce_step(3, 0)),
+        ("pass_3", lambda: pass_on(3) if H > 3 else None),
+        ("pass_last", lambda: pass_on(H)),
+        ("send_back_rows", lambda: send_rows(1)),
         ("gather2_wait1", lambda: gather_wait(2, 1)),
         ("gather2_send2", lambda: gather_on(2, 2)),
+        ("reduce3a", lambda: reduce_step(3, 0)),
         ("reduce3b", lambda: reduce_step(3, 1)),
-        ("send_back_rows", lambda: send_rows(1)),
         ("hand_over", hand_over),
         ("wait_back_rows", lambda: wait_rows(1)),
         ("key_value", key_value),
-        ("handed_own", handed_own),
+        ("handed_own", lambda: handed(True)),
         ("gather2_wait2", lambda: gather_on(2, 2, True)),
         ("weight_own", lambda: weight_product(own_rows, True)),
         ("mixed_done", mixed_done),
-        ("handed_over", handed_over),
+        ("handed_over", lambda: handed(False)),
         ("weight_other", lambda: weight_product(other_rows, False)),
         ("drain", drain),
     ]
@@ -692,17 +660,12 @@
 
 
 def finish(*refs):
-    count = len(refs) // 3
-    given, made, held = refs[:count], refs[count : 2 * count], refs[2 * count : 3 * count]
-    in_sem, out_sem = refs[3 * count :]
-    ins = [pltpu.make_async_copy(a, b, in_sem.at[n]) for n, (a, b) in enumerate(zip(given, held))]
-    outs = [pltpu.make_async_copy(a, b, out_sem.at[n]) for n, (a, b) in enumerate(zip(held, made))]
-    for one in ins:
+    count = len(refs) // 2
+    given, made, sem = refs[:count], refs[count : 2 * count], refs[-1]
+    copies = [pltpu.make_async_copy(a, b, sem.at[n]) for n, (a, b) in enumerate(zip(given, made))]
+    for one in copies:
         one.start()
-    for one, other in zip(ins, outs):
-        one.wait()
-        other.start()
-    for one in outs:
+    for one in copies:
         one.wait()
 
 
@@ -723,13 +686,13 @@
         results = (small, small, small, small, jax.ShapeDtypeStruct((C, C), BF16))
         made = pl.pallas_call(
             functools.partial(body, X, Y, Z),
-            out_shape=results,
+            out_shape=tuple(pltpu.VMEM(one.shape, BF16) for one in results),
             in_specs=[anywhere] * 9,
-            out_specs=(anywhere,) * 5,
+            out_specs=(pl.BlockSpec(memory_space=pltpu.VMEM),) * 5,
             scratch_shapes=[
                 pltpu.VMEM((2 * Z, C, C), BF16),
                 pltpu.VMEM((2 * Z, R, C), BF16),
-                pltpu.VMEM((X, Y, R, C), BF16),
+                pltpu.VMEM((N, R, C), BF16),
                 pltpu.VMEM((X, Y, R, C), BF16),
                 pltpu.VMEM((2 * Z, R, C), BF16),
                 pltpu.VMEM((Z, R, C), BF16),
@@ -757,34 +720,27 @@
                 pltpu.VMEM((M, 8, C), F32),
                 pltpu.VMEM((M, 8, C), F32),
                 pltpu.VMEM((M, 8, C), F32),
-                pltpu.VMEM((R, C), BF16),
-                pltpu.VMEM((R, C), BF16),
-                pltpu.VMEM((R, C), BF16),
-                pltpu.VMEM((R, C), BF16),
-                pltpu.VMEM((C, C), BF16),
-                dma((5,)),
-                dma((2 * Z,)),
+                dma((1,)),
+                dma((1,)),
                 dma((2, H, 2)),
-                dma((2, H, 2)),
+                dma((1,)),
+                dma((2,)),
+                dma((1,)),
+                dma((X,)),
+                dma((1,)),
+                dma((2,)),
+                dma((1,)),
+                dma((2, X)),
+                dma((2,)),
+                dma((2,)),
+                dma((2,)),
+                dma((2,)),
+                dma((1,)),
+                dma((top,)),
+                dma((top,)),
+                dma((1,)),
                 dma((Z,)),
-                dma((Z,)),
-                dma((Z,)),
-                dma((N,)),
-                dma((2, N)),
-                dma((2, N)),
-                dma((2, N)),
-                dma((2, N)),
-                dma((2, Y)),
-                dma((2, Y)),
-                dma((2, X)),
-                dma((2, X)),
-                dma((2, 2, top)),
-                dma((2, 2, top)),
-                dma((2, 2, top)),
-                dma((2, 2, top)),
-                dma((Z,)),
-                dma((Z,)),
-                dma((2, H, 2)),
+                dma((1,)),
                 dma((2, H, 2)),
             ],
             compiler_params=pltpu.CompilerParams(
@@ -797,8 +753,8 @@
             out_shape=results,
             in_specs=[anywhere] * 5,
             out_specs=(anywhere,) * 5,
-            scratch_shapes=[pltpu.VMEM(one.shape, BF16) for one in results] + [dma((5,)), dma((5,))],
-            compiler_params=pltpu.CompilerParams(vmem_limit_bytes=56 * 1024 * 1024),
+            scratch_shapes=[dma((5,))],
+            compiler_params=pltpu.CompilerParams(vmem_limit_bytes=1024 * 1024),
             name="hand_out",
         )(*made)
 

time: 57.2 us -> 51.9 us (0.907)
  the two profiles are of different devices: /device:TPU:96 before, /device:TPU:64 now
where the time goes in v2:
time: 51.9 us; the launch traced here: 51.8 us
  Pallas kernels  51.2 us (99%)
  between operations  0.64 us (1%)
    pallas_call x1, Pallas kernels, shards(): pl.pallas_call(functools.partial(body, X, Y, Z), out_shape=tuple((pltpu.V...  50.2 us

profile of v2, /device:TPU:64, one launch (start us, length us, event | category | flops | bytes accessed | tf_op | source)
XLA Modules:
  0.0 51.8 jit_solution(13931907640567692852)
XLA Ops:
  0.6 50.2 %hyena_block.1 = (bf16[128,512]{1,0:T(8,128)(2,1)S(1)}, bf16[128,512]{1,0:T(8,128)(2,1)S(1)}, bf16[128,512]{1,0:T(8,128)(2,1)S(1)}, bf16[128,512]{1,0:T(8,128)(2,1)S(1)}, bf16[512,512]{1,0:T(8,128)(2,1)S(1)}) custom-call(bf16[128,512]{1,0:T(8,128)(2,1)} %q_in.1, bf16[128,512]{1,0:T(8,128)(2,1)} %k_in.1, bf16[128,512]{1,0:T(8,128)(2,1)} %v_in.1, ...), custom_call_target="tpu_custom_call" | custom-call | tf_op jit(solution)/shard_map/hyena_block/pallas_call | solution.py:687
  50.8 1.0 %hand_out.1 = (bf16[128,512]{1,0:T(8,128)(2,1)}, bf16[128,512]{1,0:T(8,128)(2,1)}, bf16[128,512]{1,0:T(8,128)(2,1)}, bf16[128,512]{1,0:T(8,128)(2,1)}, bf16[512,512]{1,0:T(8,128)(2,1)}) custom-call(bf16[128,512]{1,0:T(8,128)(2,1)S(1)} %get-tuple-element.10.refs_0_, bf16[128,512]{1,0:T(8,128)(2,1)S(1)} %get-tuple-element.11.refs_1_, ...), custom_call_target="tpu_custom_call" | custom-call | tf_op jit(solution)/shard_map/hand_out/pallas_call | solution.py:751

commit v3 on v2

--- a/solution.py
+++ b/solution.py
@@ -317,17 +317,15 @@
 
     half = R // 2
 
-    def g1_copy(part_at, way, hop, sending):
-        size, last, devices, at = (X, X // 2, xdev, cx) if part_at == 0 else (Y, Y // 2, ydev, cy)
-        away = hop - 1 if sending else hop
-        owner = (at - away + size) % size if way == 0 else (at + away) % size
-        low = part_at * half
-        if hop == last:
-            rows = pl.ds(low + way * (half // 2), half // 2)
-        else:
-            rows = pl.ds(low, half)
-        ref = gat.at[owner, cy, rows] if part_at == 0 else gat.at[cx, owner, rows]
-        return copy(ref, ref, ga_ss.at[0], g1_rs.at[hop - 1], devices[way])
+    def gather_first():
+        for part_at in range(2):
+            ref = gat.at[cx, cy, pl.ds(part_at * half, half)]
+            for away in range(1, X):
+                to = ((cx + away) % X) * Y + cy if part_at == 0 else cx * Y + (cy + away) % Y
+                copy(ref, ref, ga_ss.at[0], g1_rs.at[0], (to, j)).start()
+
+    def gather_first_here():
+        arrived(g1_rs.at[0], gat.at[0, pl.ds(0, X - 1)])
 
     def g2_copy(part_at, way, hop, sending):
         size, last, devices, at, many = (
@@ -340,30 +338,22 @@
         ref = gat.at[group, owner, rows] if part_at == 0 else gat.at[owner, group, rows]
         return copy(ref, ref, ga_ss.at[0], g2_rs.at[hop - 1], devices[way])
 
-    def hops_of(phase, part_at):
-        return (X // 2, Y // 2)[part_at if phase == 1 else 1 - part_at]
-
-    def gather_send(phase, hop):
-        make = g1_copy if phase == 1 else g2_copy
-        for part_at in range(2):
-            if hop <= hops_of(phase, part_at):
+    def gather_send(hop):
+        if hop <= X // 2:
+            for part_at in range(2):
                 for way in range(2):
-                    make(part_at, way, hop, True).start()
-
-    def gather_wait(phase, hop):
-        count = 2 if hop < X // 2 else 1
-        if phase == 1:
-            arrived(g1_rs.at[hop - 1], gat.at[0, pl.ds(0, count)])
-        else:
-            arrived(g2_rs.at[hop - 1], gat.at[pl.ds(0, count)])
+                    g2_copy(part_at, way, hop, True).start()
+
+    def gather_wait(hop):
+        if hop <= X // 2:
+            arrived(g2_rs.at[hop - 1], gat.at[pl.ds(0, 2 if hop < X // 2 else 1)])
 
     def sb_copy(zz, sending):
         target = zz * 2 + (1 - r if sending else r)
         return copy(part.at[target], sib.at[zz], sb_ss.at[0], sb_rs.at[zz], sibling)
 
     def project(lo, hi):
-        @pl.loop(lo, hi)
-        def _(o):
+        for o in range(lo, hi):
             hop = H - (o + 1) // 2
             zz = (z + Z + hop * (2 * (o % 2) - 1)) % Z
             gated = gat[cx, cy]
@@ -452,7 +442,6 @@
         group_arrived(n)
         for way in range(2):
             ex_copy(way, n, True).start()
-        fw_copy(True, n).start()
 
     reach = (z - c // 2 + Z) % Z
 
@@ -463,6 +452,12 @@
         def _():
             cot_t[c, own_rows] = cot_all[c, own_rows]
             pl.loop(0, X)(pass_group)
+
+    def hand_own():
+        @pl.when(active)
+        def _():
+            for n in range(X):
+                fw_copy(True, n).start()
 
     def hand_group(n):
         for way in range(2):
@@ -512,7 +507,7 @@
         carry_in(True)
         add_carry(True, conv)
         gat[cx, cy] = (q_ref[...].astype(F32) * conv[...]).astype(BF16)
-        gather_send(1, 1)
+        gather_first()
 
     def multiply_back(distances, cores, first=False):
         if not distances:
@@ -561,15 +556,9 @@
         left(ga_ss.at[0], cot_all.at[pl.ds(0, N - 1)])
         drain_passed()
 
-    top = max(X // 2, Y // 2)
-
     def arrive(hop, k):
         if hop < H:
             ag_arrive(hop, k)
-
-    def gather_on(phase, lo, last=False):
-        for hop in range(lo, top + 1):
-            gather_wait(phase, hop) if last else gather_send(phase, hop)
 
     assert H <= 4 and X == Y and N == 2 * Z
     def scatter_at(away):
@@ -607,37 +596,35 @@
         ("arrive3b", lambda: arrive(3, 1)),
         ("reduce_first", reduce_first),
         ("scatter3", lambda: scatter_at(3) if H > 3 else None),
-        ("gather1_wait1", lambda: gather_wait(1, 1)),
-        ("gather1_send2", lambda: gather_on(1, 2)),
         ("sibling_near", lambda: sibling_here(0)),
         ("back_near", lambda: multiply_back(near, both, True)),
-        ("pass_0", lambda: pass_on(0)),
+        ("gather1", gather_first_here),
+        ("gather2_send1", lambda: gather_send(1)),
         ("arrive_last", lambda: (ag_arrive(H, 0), ag_arrive(H, 1))),
         ("scatter_last", lambda: scatter_at(H)),
+        ("back_far_same", lambda: multiply_back(far, same)),
         ("reduce_second", reduce_second),
-        ("back_far_same", lambda: multiply_back(far, same)),
-        ("pass_1", lambda: pass_on(1) if H > 1 else None),
-        ("gather1_wait2", lambda: gather_on(1, 2, True)),
-        ("gather2_send1", lambda: gather_send(2, 1)),
-        ("pass_2", lambda: pass_on(2) if H > 2 else None),
+        ("pass_01", lambda: pass_on(*range(min(2, H)))),
         ("sibling_far", lambda: sibling_here(1)),
         ("back_far_other", lambda: multiply_back(far, (1 - r,))),
         ("back_states", back_states),
+        ("pass_2", lambda: pass_on(2) if H > 2 else None),
+        ("pass_3", lambda: pass_on(3) if H > 3 else None),
         ("reduce2a", lambda: reduce_step(2, 0)),
         ("correlate", lambda: convolve(cgr, False, mix)),
         ("reduce2b", lambda: reduce_step(2, 1)),
-        ("pass_3", lambda: pass_on(3) if H > 3 else None),
         ("pass_last", lambda: pass_on(H)),
+        ("gather2_wait1", lambda: gather_wait(1)),
+        ("gather2_send2", lambda: gather_send(2)),
         ("send_back_rows", lambda: send_rows(1)),
-        ("gather2_wait1", lambda: gather_wait(2, 1)),
-        ("gather2_send2", lambda: gather_on(2, 2)),
+        ("hand_own", hand_own),
         ("reduce3a", lambda: reduce_step(3, 0)),
         ("reduce3b", lambda: reduce_step(3, 1)),
         ("hand_over", hand_over),
         ("wait_back_rows", lambda: wait_rows(1)),
         ("key_value", key_value),
         ("handed_own", lambda: handed(True)),
-        ("gather2_wait2", lambda: gather_on(2, 2, True)),
+        ("gather2_wait2", lambda: gather_wait(2)),
         ("weight_own", lambda: weight_product(own_rows, True)),
         ("mixed_done", mixed_done),
         ("handed_over", lambda: handed(False)),
@@ -736,7 +723,7 @@
                 dma((2,)),
                 dma((2,)),
                 dma((1,)),
-                dma((top,)),
+                dma((1,)),
                 dma((top,)),
                 dma((1,)),
                 dma((Z,)),

time: 51.9 us -> 50.1 us (0.965)
  the two profiles are of different devices: /device:TPU:64 before, /device:TPU:32 now
where the time goes in v3:
time: 50.1 us
  Pallas kernels  49.4 us (99%)
  between operations  0.64 us (1%)
    pallas_call x1, Pallas kernels, shards(): pl.pallas_call(functools.partial(body, X, Y, Z), out_shape=tuple((pltpu.V...  48.4 us
    pallas_call x1, Pallas kernels, shards(): pl.pallas_call(finish, out_shape=results, in_specs=[anywhere] * 5, out_sp...  1.01 us

profile of v3, /device:TPU:32, one launch (start us, length us, event | category | flops | bytes accessed | tf_op | source)
XLA Modules:
  0.0 50.1 jit_solution(18136210685918412019)
XLA Ops:
  0.6 48.4 %hyena_block.1 = (bf16[128,512]{1,0:T(8,128)(2,1)S(1)}, bf16[128,512]{1,0:T(8,128)(2,1)S(1)}, bf16[128,512]{1,0:T(8,128)(2,1)S(1)}, bf16[128,512]{1,0:T(8,128)(2,1)S(1)}, bf16[512,512]{1,0:T(8,128)(2,1)S(1)}) custom-call(bf16[128,512]{1,0:T(8,128)(2,1)} %q_in.1, bf16[128,512]{1,0:T(8,128)(2,1)} %k_in.1, bf16[128,512]{1,0:T(8,128)(2,1)} %v_in.1, ...), custom_call_target="tpu_custom_call" | custom-call | tf_op jit(solution)/shard_map/hyena_block/pallas_call | solution.py:674
  49.0 1.0 %hand_out.1 = (bf16[128,512]{1,0:T(8,128)(2,1)}, bf16[128,512]{1,0:T(8,128)(2,1)}, bf16[128,512]{1,0:T(8,128)(2,1)}, bf16[128,512]{1,0:T(8,128)(2,1)}, bf16[512,512]{1,0:T(8,128)(2,1)}) custom-call(bf16[128,512]{1,0:T(8,128)(2,1)S(1)} %get-tuple-element.10.refs_0_, bf16[128,512]{1,0:T(8,128)(2,1)S(1)} %get-tuple-element.11.refs_1_, ...), custom_call_target="tpu_custom_call" | custom-call | tf_op jit(solution)/shard_map/hand_out/pallas_call | solution.py:738

commit v4 on v3

--- a/solution.py
+++ b/solution.py
@@ -584,12 +584,11 @@
         ("arrive1b", lambda: arrive(1, 1)),
         ("wait_rows", lambda: wait_rows(0)),
         ("gate", gate),
-        ("scatter01", lambda: scatter(-min(1, H - 1), min(1, H - 1) + 1)),
         ("arrive2a", lambda: arrive(2, 0)),
         ("wait_weights", wait_weights),
         ("project_1", projects(0, 3)),
         ("arrive2b", lambda: arrive(2, 1)),
-        ("scatter2", lambda: scatter_at(2) if H > 2 else None),
+        ("scatter_near", lambda: scatter(near[0], near[-1] + 1)),
         ("project_2", projects(3, 5)),
         ("arrive3a", lambda: arrive(3, 0)),
         ("project_3", projects(5, Z)),
@@ -598,10 +597,10 @@
         ("scatter3", lambda: scatter_at(3) if H > 3 else None),
         ("sibling_near", lambda: sibling_here(0)),
         ("back_near", lambda: multiply_back(near, both, True)),
+        ("arrive_last", lambda: (ag_arrive(H, 0), ag_arrive(H, 1))),
+        ("scatter_last", lambda: scatter_at(H)),
         ("gather1", gather_first_here),
         ("gather2_send1", lambda: gather_send(1)),
-        ("arrive_last", lambda: (ag_arrive(H, 0), ag_arrive(H, 1))),
-        ("scatter_last", lambda: scatter_at(H)),
         ("back_far_same", lambda: multiply_back(far, same)),
         ("reduce_second", reduce_second),
         ("pass_01", lambda: pass_on(*range(min(2, H)))),

time: 50.1 us -> 49.5 us (0.988)
  the two profiles are of different devices: /device:TPU:32 before, /device:TPU:64 now
where the time goes in v4:
time: 49.5 us
  Pallas kernels  48.8 us (99%)
  between operations  0.64 us (1%)
    pallas_call x1, Pallas kernels, shards(): pl.pallas_call(functools.partial(body, X, Y, Z), out_shape=tuple((pltpu.V...  47.8 us
    pallas_call x1, Pallas kernels, shards(): pl.pallas_call(finish, out_shape=results, in_specs=[anywhere] * 5, out_sp...  1.01 us

profile of v4, /device:TPU:64, one launch (start us, length us, event | category | flops | bytes accessed | tf_op | source)
XLA Modules:
  0.0 49.5 jit_solution(5877237348805011021)
XLA Ops:
  0.6 47.8 %hyena_block.1 = (bf16[128,512]{1,0:T(8,128)(2,1)S(1)}, bf16[128,512]{1,0:T(8,128)(2,1)S(1)}, bf16[128,512]{1,0:T(8,128)(2,1)S(1)}, bf16[128,512]{1,0:T(8,128)(2,1)S(1)}, bf16[512,512]{1,0:T(8,128)(2,1)S(1)}) custom-call(bf16[128,512]{1,0:T(8,128)(2,1)} %q_in.1, bf16[128,512]{1,0:T(8,128)(2,1)} %k_in.1, bf16[128,512]{1,0:T(8,128)(2,1)} %v_in.1, ...), custom_call_target="tpu_custom_call" | custom-call | tf_op jit(solution)/shard_map/hyena_block/pallas_call | solution.py:673
  48.5 1.0 %hand_out.1 = (bf16[128,512]{1,0:T(8,128)(2,1)}, bf16[128,512]{1,0:T(8,128)(2,1)}, bf16[128,512]{1,0:T(8,128)(2,1)}, bf16[128,512]{1,0:T(8,128)(2,1)}, bf16[512,512]{1,0:T(8,128)(2,1)}) custom-call(bf16[128,512]{1,0:T(8,128)(2,1)S(1)} %get-tuple-element.10.refs_0_, bf16[128,512]{1,0:T(8,128)(2,1)S(1)} %get-tuple-element.11.refs_1_, ...), custom_call_target="tpu_custom_call" | custom-call | tf_op jit(solution)/shard_map/hand_out/pallas_call | solution.py:737

commit v5 on v4

--- a/solution.py
+++ b/solution.py
@@ -613,10 +613,10 @@
         ("correlate", lambda: convolve(cgr, False, mix)),
         ("reduce2b", lambda: reduce_step(2, 1)),
         ("pass_last", lambda: pass_on(H)),
+        ("hand_own", hand_own),
         ("gather2_wait1", lambda: gather_wait(1)),
         ("gather2_send2", lambda: gather_send(2)),
         ("send_back_rows", lambda: send_rows(1)),
-        ("hand_own", hand_own),
         ("reduce3a", lambda: reduce_step(3, 0)),
         ("reduce3b", lambda: reduce_step(3, 1)),
         ("hand_over", hand_over),

time: 49.5 us -> 49.5 us (level)
  no operation moved by 1% of the time
where the time goes in v5:
time: 49.5 us
  Pallas kernels  48.8 us (99%)
  between operations  0.64 us (1%)
    pallas_call x1, Pallas kernels, shards(): pl.pallas_call(functools.partial(body, X, Y, Z), out_shape=tuple((pltpu.V...  47.8 us
    pallas_call x1, Pallas kernels, shards(): pl.pallas_call(finish, out_shape=results, in_specs=[anywhere] * 5, out_sp...  1.01 us

profile of v5, /device:TPU:64, one launch (start us, length us, event | category | flops | bytes accessed | tf_op | source)
XLA Modules:
  0.0 49.5 jit_solution(4145305740692551509)
XLA Ops:
  0.6 47.8 %hyena_block.1 = (bf16[128,512]{1,0:T(8,128)(2,1)S(1)}, bf16[128,512]{1,0:T(8,128)(2,1)S(1)}, bf16[128,512]{1,0:T(8,128)(2,1)S(1)}, bf16[128,512]{1,0:T(8,128)(2,1)S(1)}, bf16[512,512]{1,0:T(8,128)(2,1)S(1)}) custom-call(bf16[128,512]{1,0:T(8,128)(2,1)} %q_in.1, bf16[128,512]{1,0:T(8,128)(2,1)} %k_in.1, bf16[128,512]{1,0:T(8,128)(2,1)} %v_in.1, ...), custom_call_target="tpu_custom_call" | custom-call | tf_op jit(solution)/shard_map/hyena_block/pallas_call | solution.py:673
  48.5 1.0 %hand_out.1 = (bf16[128,512]{1,0:T(8,128)(2,1)}, bf16[128,512]{1,0:T(8,128)(2,1)}, bf16[128,512]{1,0:T(8,128)(2,1)}, bf16[128,512]{1,0:T(8,128)(2,1)}, bf16[512,512]{1,0:T(8,128)(2,1)}) custom-call(bf16[128,512]{1,0:T(8,128)(2,1)S(1)} %get-tuple-element.10.refs_0_, bf16[128,512]{1,0:T(8,128)(2,1)S(1)} %get-tuple-element.11.refs_1_, ...), custom_call_target="tpu_custom_call" | custom-call | tf_op jit(solution)/shard_map/hand_out/pallas_call | solution.py:737
